TPU v7x, 32 devices: a whole 2x2x4 slice. The times are simulated.
32 devices in a mesh: nodes: 8 (over z, y), heads: 4 (over x, core).
Axes of the slice: x: 2, y: 2, z: 4, core: 2. Of those that a mesh axis runs over, the one named last changes fastest.
Arguments:
- node_feats: bfloat16 [2048, 512], P('nodes'), may hold values from -6 to 6
- node_types: int32 [2048], P('nodes'), may hold values from 0 to 4
- queries: bfloat16 [2048, 512], P('nodes', 'heads'), may hold values from -6 to 6
- key_rows: bfloat16 [2048, 512], P('nodes', 'heads'), may hold values from -6 to 6
- value_rows: bfloat16 [2048, 512], P('nodes', 'heads'), may hold values from -6 to 6
- halo_keys: bfloat16 [512, 512], P('nodes', 'heads'), may hold values from -6 to 6
- halo_values: bfloat16 [512, 512], P('nodes', 'heads'), may hold values from -6 to 6
- halo_rows: int32 [512], P('nodes'), may hold values from 0 to 256, as said below
- edge_tiles: int32 [320, 3], P('nodes'), may hold values from 0 to 14, as said below
- grad_output: bfloat16 [2048, 512], P('nodes', 'heads'), may hold values from -6 to 6
- proj_weight: bfloat16 [3, 5, 512, 512], P(None, None, None, 'heads'), may hold values from -0.25 to 0.25
- rel_weight: bfloat16 [2, 15, 8, 64, 64], P(None, None, 'heads'), may hold values from -0.75 to 0.75
- rel_prior: float32 [15, 8], P(None, 'heads'), may hold values from 0.5 to 2
Outputs:
- grad_feats: bfloat16 [2048, 512], P('nodes', 'heads')
- grad_proj: float32 [512, 3, 5, 512], P('nodes', None, None, 'heads')
- grad_rel: float32 [2, 15, 8, 64, 64], P(None, None, 'heads')
- grad_prior: float32 [15, 8], P(None, 'heads')
Inputs may be any that keep to these rules, and one draw needn't show every extreme that they name: `halo_rows`: slab s's halo is 8 blocks of 8 slots, block j holding distinct rows of slab j first and 256 in its empty slots; block s of slab s is empty; one slab t is copied in full: every slab other than t holds 8 distinct rows of t in block t; every other block of another slab holds between 1 and 8 rows. `edge_tiles`: an entry is live when its destination tile is below 4, and is empty with destination 256 // 64, source 0 and relation 0. A source tile below 4 lies among the slab's own rows, the others among its halo slots. Every destination tile has a live entry whose source lies among the own rows. Some slab has every entry live.
All inputs are finite; a program needn't handle non-finite values.
Results may differ from a plain program's by a relative error of at most 0.012.
The roundings to bfloat16 on the way count: a program that leaves them out, or rounds other values in their place, can miss the bound.
Values may be sent and summed in bfloat16 or wider, within the bound.
A program may use at most 64 MiB of HBM per device.

v0:
```python
import jax
import jax.numpy as jnp
from jax import lax
from jax.sharding import PartitionSpec as P

TYPES = 5
RELS = 15
TILE = 64


def attend(queries, key_rows, value_rows, valid, grad_output, edge_tiles, rel_weight, rel_prior):
    head_count = queries.shape[1]
    head_dim = queries.shape[2]
    dest_tiles = queries.shape[0] // TILE
    source_tiles = key_rows.shape[0] // TILE
    inv_root = head_dim ** (-0.5)
    query_tiles = queries.reshape(dest_tiles, TILE, head_count, head_dim)
    key_tiles = key_rows.reshape(source_tiles, TILE, head_count, head_dim)
    value_tiles = value_rows.reshape(source_tiles, TILE, head_count, head_dim)
    grad_tiles = grad_output.reshape(dest_tiles, TILE, head_count, head_dim)
    target = edge_tiles[:, 0]
    source = edge_tiles[:, 1]
    relation = edge_tiles[:, 2]
    live_mask = (target < dest_tiles).astype(jnp.float32)
    clipped = jnp.minimum(target, dest_tiles - 1)
    query_edge = query_tiles[clipped]
    key_edge = key_tiles[source]
    value_edge = value_tiles[source]
    grad_edge = grad_tiles[clipped]
    columns = valid.reshape(source_tiles, TILE)[source] * live_mask[:, None]
    chooser = relation[:, None] == jnp.arange(RELS)[None, :]
    chooser_bf = chooser.astype(jnp.bfloat16)
    chooser_wide = chooser.astype(jnp.float32)
    score_weight = jnp.einsum(
        "er,rhab->ehab", chooser_bf, rel_weight[0], preferred_element_type=jnp.float32
    ).astype(jnp.bfloat16)
    message_weight = jnp.einsum(
        "er,rhab->ehab", chooser_bf, rel_weight[1], preferred_element_type=jnp.float32
    ).astype(jnp.bfloat16)
    prior_edge = jnp.dot(chooser_wide, rel_prior, precision=lax.Precision.HIGHEST)
    key_mixed = jnp.einsum(
        "etha,ehab->ethb", key_edge, score_weight, preferred_element_type=jnp.float32
    ).astype(jnp.bfloat16)
    message = jnp.einsum(
        "etha,ehab->ethb", value_edge, message_weight, preferred_element_type=jnp.float32
    ).astype(jnp.bfloat16)
    logits = (
        jnp.einsum("etha,esha->ehts", query_edge, key_mixed, preferred_element_type=jnp.float32)
        * inv_root
    )
    exp_scores = jnp.exp(logits * prior_edge[:, :, None, None]) * columns[:, None, None, :]
    owner_map = (target[:, None] == jnp.arange(dest_tiles)[None, :]).astype(jnp.float32)
    denominator = jnp.einsum(
        "ed,eht->dht", owner_map, jnp.sum(exp_scores, axis=-1), precision=lax.Precision.HIGHEST
    )
    softmax = exp_scores / denominator[clipped][..., None]
    prob_bf = softmax.astype(jnp.bfloat16)
    partial_value = jnp.einsum(
        "ehts,eshb->ethb", prob_bf, message, preferred_element_type=jnp.float32
    )
    output = jnp.einsum("ed,ethb->dthb", owner_map, partial_value, precision=lax.Precision.HIGHEST)
    deltas = jnp.sum(grad_tiles.astype(jnp.float32) * output, axis=-1)
    delta_edge = jnp.transpose(deltas[clipped], (0, 2, 1))
    prob_grad = jnp.einsum(
        "ethb,eshb->ehts", grad_edge, message, preferred_element_type=jnp.float32
    )
    score_grad = softmax * (prob_grad - delta_edge[..., None])
    logit_grad = (score_grad * (prior_edge * inv_root)[:, :, None, None]).astype(jnp.bfloat16)
    query_edge_grad = jnp.einsum(
        "ehts,esha->etha", logit_grad, key_mixed, preferred_element_type=jnp.float32
    )
    key_mixed_grad = jnp.einsum(
        "ehts,etha->esha", logit_grad, query_edge, preferred_element_type=jnp.float32
    ).astype(jnp.bfloat16)
    message_grad = jnp.einsum(
        "ehts,ethb->eshb", prob_bf, grad_edge, preferred_element_type=jnp.float32
    ).astype(jnp.bfloat16)
    key_edge_grad = jnp.einsum(
        "eshb,ehab->esha", key_mixed_grad, score_weight, preferred_element_type=jnp.float32
    )
    value_edge_grad = jnp.einsum(
        "eshb,ehab->esha", message_grad, message_weight, preferred_element_type=jnp.float32
    )
    score_weight_grad = jnp.einsum(
        "esha,eshb->ehab", key_edge, key_mixed_grad, preferred_element_type=jnp.float32
    )
    message_weight_grad = jnp.einsum(
        "esha,eshb->ehab", value_edge, message_grad, preferred_element_type=jnp.float32
    )
    prior_edge_grad = jnp.sum(score_grad * logits, axis=(2, 3))
    source_map = (source[:, None] == jnp.arange(source_tiles)[None, :]).astype(
        jnp.float32
    ) * live_mask[:, None]
    query_grad = jnp.einsum(
        "ed,etha->dtha", owner_map, query_edge_grad, precision=lax.Precision.HIGHEST
    )
    key_grad = jnp.einsum(
        "ej,esha->jsha", source_map, key_edge_grad, precision=lax.Precision.HIGHEST
    )
    value_grad = jnp.einsum(
        "ej,esha->jsha", source_map, value_edge_grad, precision=lax.Precision.HIGHEST
    )
    relation_grad = jnp.stack(
        [
            jnp.einsum(
                "er,ehab->rhab", chooser_wide, score_weight_grad, precision=lax.Precision.HIGHEST
            ),
            jnp.einsum(
                "er,ehab->rhab", chooser_wide, message_weight_grad, precision=lax.Precision.HIGHEST
            ),
        ]
    )
    prior_grad = jnp.einsum(
        "er,eh->rh", chooser_wide, prior_edge_grad, precision=lax.Precision.HIGHEST
    )
    return (
        query_grad.reshape(dest_tiles * TILE, head_count * head_dim),
        key_grad.reshape(source_tiles * TILE, head_count * head_dim),
        value_grad.reshape(source_tiles * TILE, head_count * head_dim),
        relation_grad,
        prior_grad,
    )


def per_device(
    node_feats,
    node_types,
    queries,
    key_rows,
    value_rows,
    halo_keys,
    halo_values,
    halo_rows,
    edge_tiles,
    grad_output,
    proj_weight,
    rel_weight,
    rel_prior,
):
    own_count = node_feats.shape[0]
    halo_count = halo_keys.shape[0]
    local_width = queries.shape[1]
    head_count = rel_prior.shape[1]
    head_dim = local_width // head_count
    feature_count = node_feats.shape[1]

    def by_heads(matrix):
        return matrix.reshape(matrix.shape[0], head_count, head_dim)

    valid = jnp.concatenate(
        [jnp.ones((own_count,), jnp.float32), (halo_rows < own_count).astype(jnp.float32)]
    )
    query_grad, key_grad, value_grad, relation_grad, prior_grad = attend(
        by_heads(queries),
        by_heads(jnp.concatenate([key_rows, halo_keys])),
        by_heads(jnp.concatenate([value_rows, halo_values])),
        valid,
        by_heads(grad_output),
        edge_tiles,
        rel_weight,
        rel_prior,
    )
    outgoing = jnp.concatenate([key_grad[own_count:], value_grad[own_count:]], axis=1).astype(
        jnp.bfloat16
    )
    incoming, incoming_rows = (
        lax.all_to_all(outgoing, "nodes", split_axis=0, concat_axis=0, tiled=True),
        lax.all_to_all(halo_rows, "nodes", split_axis=0, concat_axis=0, tiled=True),
    )
    type_range = jnp.arange(TYPES)
    own_types = (node_types[:, None] == type_range[None, :]).astype(jnp.bfloat16)
    own_stack = jnp.stack(
        [query_grad, key_grad[:own_count], value_grad[:own_count]], axis=1
    ).astype(jnp.bfloat16)
    own_blocks = own_types[:, None, :, None] * own_stack[:, :, None, :]
    clamped = jnp.minimum(incoming_rows, own_count - 1)
    halo_types = (node_types[clamped][:, None] == type_range[None, :]).astype(jnp.bfloat16)
    halo_blocks = (
        halo_types[:, None, :, None] * incoming.reshape(halo_count, 2, local_width)[:, :, None, :]
    )
    contract = (((1, 2, 3), (0, 1, 3)), ((), ()))
    feat_grad = lax.dot_general(
        own_blocks, proj_weight, contract, preferred_element_type=jnp.float32
    )
    halo_feat = lax.dot_general(
        halo_blocks, proj_weight[1:], contract, preferred_element_type=jnp.float32
    )
    feat_grad = feat_grad.at[incoming_rows].add(halo_feat, mode="drop")
    grad_feats = lax.psum_scatter(feat_grad, "heads", scatter_dimension=1, tiled=True).astype(
        jnp.bfloat16
    )
    halo_feats = node_feats[clamped]
    shard_rows = feature_count // lax.axis_size("nodes")
    halo_cols = lax.slice_in_dim(halo_feats, 0, feature_count, axis=1)
    own_part = jnp.einsum(
        "ri,rptk->iptk", node_feats, own_blocks, preferred_element_type=jnp.float32
    )
    halo_part = jnp.einsum(
        "ri,rptk->iptk", halo_cols, halo_blocks, preferred_element_type=jnp.float32
    )
    summed = lax.psum(own_part.at[:, 1:].add(halo_part), "nodes")
    grad_proj = lax.dynamic_slice_in_dim(
        summed, lax.axis_index("nodes") * shard_rows, shard_rows, 0
    )
    grad_rel, grad_prior = lax.psum((relation_grad, prior_grad), "nodes")
    return (grad_feats, grad_proj, grad_rel, grad_prior)


def solution(mesh):
    return jax.shard_map(
        per_device,
        mesh=mesh,
        in_specs=(
            P("nodes", None),
            P("nodes"),
            P("nodes", "heads"),
            P("nodes", "heads"),
            P("nodes", "heads"),
            P("nodes", "heads"),
            P("nodes", "heads"),
            P("nodes"),
            P("nodes", None),
            P("nodes", "heads"),
            P(None, None, None, "heads"),
            P(None, None, "heads", None, None),
            P(None, "heads"),
        ),
        out_specs=(
            P("nodes", "heads"),
            P("nodes", None, None, "heads"),
            P(None, None, "heads", None, None),
            P(None, "heads"),
        ),
        check_vma=False,
    )
```

profile of v0, /device:TPU:0, one launch (start us, length us, event | category | flops | bytes accessed | tf_op | source)
XLA Modules:
  0.0 345.1 jit_solution(1994885721512988819)
XLA Ops:
  9.4 7.3 %all-to-all-start = ((s32[8,8,1]{1,2,0:T(1,128)}), s32[8,8,1]{1,2,0:T(1,128)S(1)}, u32[]{:S(2)}, u32[]{:S(2)}) async-start(s32[8,8,1]{1,2,0:T(1,128)} %bitcast.29), calls=%async_computation | async-start | bytes 8192 | tf_op jit(solution)/shard_map/all_to_all | solution.py:168
  20.3 2.0 fusion.92
  28.1 2.0 fusion.8
  30.8 1.8 gather_fusion.1
  32.6 3.9 %fusion.7 = (f32[40,2,64]{2,1,0:T(2,128)S(1)}, f32[40,2,64,64]{2,3,1,0:T(8,128)}) fusion(f32[40,64]{1,0:T(8,128)} %broadcast_multiply_fusion, f32[40,2]{1,0:T(8,128)S(1)} %copy.108, bf16[40,64,2,64]{3,1,2,0:T(8,128)(2,1)} %gather_fusion.1, bf16[40,64,2,64]{1,3,2,0:T(8,128)(2,1)S(1)} %copy-done.7), kind=kOutput, calls=%fused_computation.22 | convolution fusion | flops 42920960 | bytes 2652480 | tf_op jit(solution)/shard_map/etha,esha->ehts/dot_general | solution.py:48
  43.1 2.0 convolution_bitcast_fusion.3
  45.1 3.3 copy.118
  48.6 2.8 fusion.31
  52.1 1.8 gather_fusion.4
  54.0 4.5 %fusion.11 = bf16[40,64,2,64]{1,3,2,0:T(8,128)(2,1)} fusion(bf16[40,64,2,64]{3,1,2,0:T(8,128)(2,1)} %gather_fusion.4, f32[40,2,64,64]{2,3,1,0:T(8,128)} %get-tuple-element.44, f32[40,2,64]{2,1,0:T(2,128)S(1)} %copy-done.28, f32[40,64]{1,0:T(8,128)S(1)} %copy-done.25, f32[40,2]{1,0:T(8,128)S(1)} %copy-done.23), kind=kOutput, calls=%fused_computation.37 | convolution fusion | flops 43581440 | bytes 2652480 | tf_op jit(solution)/shard_map/ehts,ethb->eshb/dot_general | solution.py:75
  58.6 2.3 multiply_reduce_fusion
  62.2 2.1 convolution_bitcast_fusion.2
  64.2 2.4 fusion.93
  66.7 2.1 convolution_bitcast_fusion.1
  68.7 3.3 copy.128
  72.0 3.3 convolution_convert_fusion.7
  75.6 2.0 convolution_bitcast_fusion
  77.6 3.3 copy.134
  80.9 3.3 convolution_convert_fusion.6
  84.5 3.4 fusion.12
  87.9 3.3 copy.122
  91.2 2.7 convolution_convert_fusion.8
  97.1 1.9 fusion.24
  99.6 1.9 copy.199
  101.5 6.0 %all-to-all-start.1 = ((bf16[8,8,256]{2,1,0:T(8,128)(2,1)}), bf16[8,8,256]{2,1,0:T(8,128)(2,1)S(1)}, u32[]{:S(2)}, u32[]{:S(2)}) async-start(bf16[8,8,256]{2,1,0:T(8,128)(2,1)} %pad_maximum_fusion.4), calls=%async_computation.1 | async-start | bytes 65536 | tf_op jit(solution)/shard_map/all_to_all | solution.py:167
  109.6 4.6 %all-to-all-done.1 = bf16[8,8,256]{2,1,0:T(8,128)(2,1)S(1)} async-done(((bf16[8,8,256]{2,1,0:T(8,128)(2,1)}), bf16[8,8,256]{2,1,0:T(8,128)(2,1)S(1)}, u32[]{:S(2)}, u32[]{:S(2)}) %all-to-all-start.1) | async-done | bytes 32800 | tf_op jit(solution)/shard_map/all_to_all | solution.py:167
  114.2 2.5 fusion.32
  120.2 2.5 fusion.15
  125.0 3.9 %fusion.1 = f32[512,3,5,128]{0,3,2,1:T(8,128)} fusion(f32[512,3,5,128]{0,3,2,1:T(8,128)} %copy.199, f32[3,5,128,512]{3,2,1,0:T(8,128)} %copy-done.2, bf16[64,2,128]{2,0,1:T(8,128)(2,1)S(1)} %copy.139, bf16[64,5]{0,1:T(8,128)(2,1)S(1)} %fusion.68, bf16[64,512]{1,0:T(8,128)(2,1)S(1)} %gather_fusion.8), kind=kOutput, calls=%fused_computation.12 | convolution fusion | flops 84869120 | bytes 5341824 | tf_op jit(solution)/shard_map/ri,rptk->iptk/dot_general | solution.py:198
  129.1 19.3 %psum.23 = f32[15,2]{0,1:T(2,128)} all-reduce(f32[15,2]{0,1:T(2,128)S(1)} %fusion.51), channel_id=1, replica_groups=mesh['nodes'=8,'heads'=4] {'nodes'}, use_global_device_ids=true, to_apply=%region_7.0 | all-reduce | flops 30 | bytes 240 | tf_op jit(solution)/shard_map/psum | solution.py:205
  149.9 181.7 %all-reduce.4.cloned.1.call-done = (f32[512,3,5,128]{0,3,2,1:T(8,128)}, f32[2,15,2,64,64]{4,1,3,2,0:T(8,128)}) async-done(((f32[512,3,5,128]{0,3,2,1:T(8,128)}, f32[2,15,2,64,64]{4,1,3,2,0:T(8,128)}), (f32[512,3,5,128]{0,3,2,1:T(8,128)}, f32[2,15,2,64,64]{4,1,3,2,0:T(8,128)})) %all-reduce.4.cloned.1.call-update) | async-done | bytes 4915216 | tf_op jit(solution)/shard_map/psum | solution.py:201
  331.6 3.4 copy.148
  (146 shorter events, 36.5 us)
Async XLA Ops:
  8.0 87.5 %copy-start = (bf16[256,512]{1,0:T(8,128)(2,1)S(1)}, bf16[256,512]{1,0:T(8,128)(2,1)}, u32[]{:S(2)}) copy-start(bf16[256,512]{1,0:T(8,128)(2,1)} %param.15) | copy-start | bytes 786436
  9.4 92.1 %all-to-all-start = ((s32[8,8,1]{1,2,0:T(1,128)}), s32[8,8,1]{1,2,0:T(1,128)S(1)}, u32[]{:S(2)}, u32[]{:S(2)}) async-start(s32[8,8,1]{1,2,0:T(1,128)} %bitcast.29), calls=%async_computation | async-start | bytes 8192 | tf_op jit(solution)/shard_map/all_to_all | solution.py:168
  19.3 10.8 %copy-start.32 = (f32[40]{0:T(128)}, f32[40]{0:T(128)S(1)}, u32[]{:S(2)}) copy-start(f32[40]{0:T(128)S(1)} %fusion.83) | copy-start | bytes 484
  22.5 3.6 %copy-start.30 = (s32[1024]{0:T(1024)}, s32[1024]{0:T(1024)S(1)}, u32[]{:S(2)}) copy-start(s32[1024]{0:T(1024)S(1)} %get-tuple-element.48) | copy-start | bytes 12292
  22.5 3.6 %copy-start.35 = (f32[15,2]{0,1:T(2,128)S(1)}, f32[15,2]{0,1:T(2,128)}, u32[]{:S(2)}) copy-start(f32[15,2]{0,1:T(2,128)} %param.27) | copy-start | bytes 364
  22.5 3.9 %copy-start.26 = (bf16[256,128]{1,0:T(8,128)(2,1)S(1)}, bf16[256,128]{1,0:T(8,128)(2,1)}, u32[]{:S(2)}) copy-start(bf16[256,128]{1,0:T(8,128)(2,1)} %param.17) | copy-start | bytes 196612
  26.1 4.0 %copy-start.3 = (bf16[40,2,64,64]{3,0,2,1:T(8,128)(2,1)}, bf16[40,2,64,64]{3,0,2,1:T(8,128)(2,1)S(1)}, u32[]{:S(2)}) copy-start(bf16[40,2,64,64]{3,0,2,1:T(8,128)(2,1)S(1)} %convolution_convert_fusion.5) | copy-start | bytes 1966084
  26.3 6.3 %copy-start.22 = (f32[40,2]{1,0:T(8,128)}, f32[40,2]{1,0:T(8,128)S(1)}, u32[]{:S(2)}) copy-start(f32[40,2]{1,0:T(8,128)S(1)} %copy.108) | copy-start | bytes 964
  32.6 5.2 %copy-start.29 = (bf16[64,128]{1,0:T(8,128)(2,1)S(1)}, bf16[64,128]{1,0:T(8,128)(2,1)}, u32[]{:S(2)}) copy-start(bf16[64,128]{1,0:T(8,128)(2,1)} %param.21) | copy-start | bytes 49156
  40.4 2.7 copy-start.14
  40.4 2.7 copy-start.23
  40.4 2.7 copy-start.25
  40.4 2.7 copy-start.28
  45.1 3.3 copy-start.27
  54.0 4.6 %copy-start.15 = (f32[40,2,64,64]{2,3,1,0:T(8,128)S(1)}, f32[40,2,64,64]{2,3,1,0:T(8,128)}, u32[]{:S(2)}) copy-start(f32[40,2,64,64]{2,3,1,0:T(8,128)} %get-tuple-element.44) | copy-start | bytes 3932164
  54.0 4.6 %copy-start.17 = (bf16[40,64,2,64]{3,1,2,0:T(8,128)(2,1)S(1)}, bf16[40,64,2,64]{3,1,2,0:T(8,128)(2,1)}, u32[]{:S(2)}) copy-start(bf16[40,64,2,64]{3,1,2,0:T(8,128)(2,1)} %gather_fusion.4) | copy-start | bytes 1966084
  54.0 4.6 %copy-start.19 = (bf16[40,64,2,64]{1,3,2,0:T(8,128)(2,1)S(1)}, bf16[40,64,2,64]{1,3,2,0:T(8,128)(2,1)}, u32[]{:S(2)}) copy-start(bf16[40,64,2,64]{1,3,2,0:T(8,128)(2,1)} %copy-done.18) | copy-start | bytes 1966084
  64.2 2.4 copy-start.4
  68.7 3.3 copy-start.31
  68.7 3.3 copy-start.33
  72.0 3.6 %copy-start.6 = (bf16[40,2,64,64]{3,0,2,1:T(8,128)(2,1)S(1)}, bf16[40,2,64,64]{3,0,2,1:T(8,128)(2,1)}, u32[]{:S(2)}) copy-start(bf16[40,2,64,64]{3,0,2,1:T(8,128)(2,1)} %copy-done.5) | copy-start | bytes 1966084
  72.0 3.6 %copy-start.11 = (bf16[40,64,2,64]{1,3,2,0:T(8,128)(2,1)S(1)}, bf16[40,64,2,64]{1,3,2,0:T(8,128)(2,1)}, u32[]{:S(2)}) copy-start(bf16[40,64,2,64]{1,3,2,0:T(8,128)(2,1)} %fusion.11) | copy-start | bytes 1966084
  80.9 3.6 %copy-start.10 = (f32[40,2,64,64]{3,2,1,0:T(8,128)S(1)}, f32[40,2,64,64]{3,2,1,0:T(8,128)}, u32[]{:S(2)}) copy-start(f32[40,2,64,64]{3,2,1,0:T(8,128)} %fusion.93) | copy-start | bytes 3932164
  84.2 3.7 %copy-start.20 = (bf16[5,64,2,64]{3,0,2,1:T(8,128)(2,1)}, bf16[5,64,2,64]{3,0,2,1:T(8,128)(2,1)S(1)}, u32[]{:S(2)}) copy-start(bf16[5,64,2,64]{3,0,2,1:T(8,128)(2,1)S(1)} %convolution_convert_fusion.6) | copy-start | bytes 245764
  91.2 3.0 slice-start.1
  91.2 3.2 slice-start
  91.2 3.6 %copy-start.1 = (s32[256]{0:T(256)S(1)}, s32[256]{0:T(256)}, u32[]{:S(2)}) copy-start(s32[256]{0:T(256)} %param.16) | copy-start | bytes 3076
  97.1 2.5 copy-start.2
  101.5 12.7 %all-to-all-start.1 = ((bf16[8,8,256]{2,1,0:T(8,128)(2,1)}), bf16[8,8,256]{2,1,0:T(8,128)(2,1)S(1)}, u32[]{:S(2)}, u32[]{:S(2)}) async-start(bf16[8,8,256]{2,1,0:T(8,128)(2,1)} %pad_maximum_fusion.4), calls=%async_computation.1 | async-start | bytes 65536 | tf_op jit(solution)/shard_map/all_to_all | solution.py:167
  107.5 40.9 %reduce-scatter.2.cloned.1.call-start = ((), (), s32[]{:S(2)}) async-start(), calls=%async_computation.3 | async-start | bytes 655360 | tf_op jit(solution)/shard_map/reduce_scatter | solution.py:189
  119.1 212.5 %all-reduce.4.cloned.1.call-start = ((), (), s32[]{:S(2)}) async-start(), calls=%async_computation.4 | async-start | bytes 12058624 | tf_op jit(solution)/shard_map/psum | solution.py:201
  120.2 2.5 copy-start.13
  (10 other events, 14.9 us)
Sparse Core Ops, SparseCore 0:
  119.2 19.0 reduce-scatter.1
Sparse Core Ops, SparseCore 1:
  129.0 202.5 all-reduce.3
where the time goes:
time: 346 us; the launch traced here: 345 us
  waiting for transfers between devices  186 us (54%)
  matrix products  55.5 us (16%)
  local copies, waits for them, and re-layouts  43.4 us (13%)
  blocking collectives  19.3 us (6%)
  between operations  16 us (5%)
  starting transfers between devices  13.6 us (4%)
  other arithmetic  11.1 us (3%)
    psum x1, waiting for transfers between devices, per_device(): summed = lax.psum(own_part.at[:, 1:].add(halo_part), 'nodes')  182 us
    psum x1, blocking collectives, per_device(): grad_rel, grad_prior = lax.psum((relation_grad, prior_grad), 'nodes')  19.3 us
    unnamed x75, local copies, waits for them, and re-layouts  10.9 us
    all_to_all x1, starting transfers between devices, per_device(): lax.all_to_all(halo_rows, 'nodes', split_axis=0, concat_axis=0, tiled=True)  7.28 us
  transfers between devices with their start and end apart: 4, of which 2 were waited for; matrix products, arithmetic and copies ran while one was open for 27% of the time, Pallas kernels for 0%

commit v1 on v0

v1 whole, which is shorter than its diff:
```python
import functools

import jax
import jax.numpy as jnp
from jax import lax
from jax.experimental import pallas as pl
from jax.experimental.pallas import tpu as pltpu
from jax.sharding import PartitionSpec as P

TYPES = 5
RELS = 15
TILE = 64
CAP = 8
BF = jnp.bfloat16
F32 = jnp.float32
VMEM = pl.BlockSpec(memory_space=pltpu.VMEM)
SMEM = pl.BlockSpec(memory_space=pltpu.SMEM)


def mm(left, right, left_dim, right_dim):
    return lax.dot_general(
        left, right, (((left_dim,), (right_dim,)), ((), ())), preferred_element_type=F32
    )


def attend_kernel(
    dest_tiles,
    source_tiles,
    edge_count,
    unroll,
    edge_ref,
    prior_ref,
    query_ref,
    key_ref,
    value_ref,
    halo_key_ref,
    halo_value_ref,
    grad_ref,
    valid_ref,
    weight_ref,
    query_out,
    key_out,
    value_out,
    rel_out,
    prior_out,
    keys,
    values,
    wide,
    mixed,
    message,
    logits,
    scores,
    prob_grad,
    sums,
    deltas,
    query_acc,
    key_acc,
    value_acc,
):
    own = dest_tiles * TILE
    width = 2 * TILE
    keys[:own] = key_ref[...]
    keys[own:] = halo_key_ref[...]
    values[:own] = value_ref[...]
    values[own:] = halo_value_ref[...]
    blank = jnp.zeros((TILE, TILE), BF)
    for side in range(2):
        for rel in range(RELS):
            wide[side, rel] = jnp.concatenate(
                [
                    jnp.concatenate([weight_ref[side, rel, 0], blank], axis=1),
                    jnp.concatenate([blank, weight_ref[side, rel, 1]], axis=1),
                ],
                axis=0,
            )
    for ref in (sums, deltas, query_acc, key_acc, value_acc, rel_out, prior_out):
        ref[...] = jnp.zeros_like(ref)
    first = lax.broadcasted_iota(jnp.int32, (TILE, width), 1) < TILE
    first_row = lax.broadcasted_iota(jnp.int32, (1, width), 1) < TILE
    low = first.astype(F32).astype(BF)
    high = (1.0 - first.astype(F32)).astype(BF)

    def stacked(both):
        return jnp.concatenate([both * low, both * high], axis=0)

    def diagonal(square):
        return jnp.where(first, square[:TILE], square[TILE:])

    def head_sum(total):
        left = jnp.sum(jnp.where(first, total, 0.0), axis=1, keepdims=True)
        right = jnp.sum(jnp.where(first, 0.0, total), axis=1, keepdims=True)
        return jnp.where(first, left, right)

    def entry(index):
        target = edge_ref[3 * index]
        live = target < dest_tiles
        dest = jnp.minimum(target, dest_tiles - 1)
        source = edge_ref[3 * index + 1]
        rel = edge_ref[3 * index + 2]
        prior = jnp.where(first_row, prior_ref[2 * rel], prior_ref[2 * rel + 1])
        return live, dest, source, rel, prior

    def rows_of(tile):
        return pl.ds(pl.multiple_of(tile * TILE, TILE), TILE)

    def score_step(step, carry):
        found = []
        for part in range(unroll):
            index = step * unroll + part
            live, dest, source, rel, prior = entry(index)
            at = rows_of(dest)
            mixed_now = mm(keys[rows_of(source)], wide[0, rel], 1, 0).astype(BF)
            message_now = mm(values[rows_of(source)], wide[1, rel], 1, 0).astype(BF)
            logit = mm(query_ref[at], stacked(mixed_now), 1, 1) * (TILE**-0.5)
            grad = mm(grad_ref[at], stacked(message_now), 1, 1)
            keep = valid_ref[source][:1] * jnp.where(live, 1.0, 0.0)
            score = jnp.where(keep > 0.0, jnp.exp(logit * prior), 0.0)
            found.append((index, dest, mixed_now, message_now, logit, grad, score))
        for index, dest, mixed_now, message_now, logit, grad, score in found:
            mixed[index] = mixed_now
            message[index] = message_now
            logits[index] = logit
            prob_grad[index] = grad
            scores[index] = score
            sums[dest] += score
        return carry

    lax.fori_loop(0, edge_count // unroll, score_step, 0)
    for tile in range(dest_tiles):
        sums[tile] = 1.0 / head_sum(sums[tile])

    def delta_step(step, carry):
        found = []
        for part in range(unroll):
            index = step * unroll + part
            _, dest, _, _, _ = entry(index)
            soft = scores[index] * sums[dest]
            found.append((index, dest, soft, soft.astype(BF).astype(F32) * prob_grad[index]))
        for index, dest, soft, product in found:
            scores[index] = soft
            deltas[dest] += product
        return carry

    lax.fori_loop(0, edge_count // unroll, delta_step, 0)
    for tile in range(dest_tiles):
        deltas[tile] = head_sum(deltas[tile])

    def grad_step(step, carry):
        found = []
        for part in range(unroll):
            index = step * unroll + part
            _, dest, source, rel, prior = entry(index)
            at = rows_of(dest)
            soft = scores[index]
            score_grad = soft * (prob_grad[index] - deltas[dest])
            prior_now = jnp.sum(score_grad * logits[index], axis=0, keepdims=True)
            logit_grad = (score_grad * (prior * (TILE**-0.5))).astype(BF)
            query_now = mm(logit_grad, stacked(mixed[index]), 1, 0)
            mixed_grad = diagonal(mm(logit_grad, query_ref[at], 0, 0)).astype(BF)
            message_grad = diagonal(mm(soft.astype(BF), grad_ref[at], 0, 0)).astype(BF)
            key_now = mm(mixed_grad, wide[0, rel], 1, 1)
            value_now = mm(message_grad, wide[1, rel], 1, 1)
            score_weight = diagonal(mm(keys[rows_of(source)], mixed_grad, 0, 0))
            message_weight = diagonal(mm(values[rows_of(source)], message_grad, 0, 0))
            found.append(
                (
                    dest,
                    source,
                    rel,
                    prior_now,
                    query_now,
                    key_now,
                    value_now,
                    score_weight,
                    message_weight,
                )
            )
        for dest, source, rel, prior_now, query_now, key_now, value_now, one, two in found:
            prior_out[rel] += prior_now
            query_acc[dest] += query_now
            key_acc[source] += key_now
            value_acc[source] += value_now
            rel_out[0, rel] += one
            rel_out[1, rel] += two
        return carry

    lax.fori_loop(0, edge_count // unroll, grad_step, 0)
    for tile in range(dest_tiles):
        query_out[tile * TILE : (tile + 1) * TILE] = query_acc[tile].astype(BF)
    for tile in range(source_tiles):
        key_out[tile * TILE : (tile + 1) * TILE] = key_acc[tile].astype(BF)
        value_out[tile * TILE : (tile + 1) * TILE] = value_acc[tile].astype(BF)


def attend(
    queries,
    key_rows,
    value_rows,
    halo_keys,
    halo_values,
    halo_rows,
    grad_output,
    edge_tiles,
    rel_weight,
    rel_prior,
):
    own, width = queries.shape
    halo = halo_keys.shape[0]
    edges = edge_tiles.shape[0]
    dest_tiles = own // TILE
    source_tiles = (own + halo) // TILE
    unroll = 4 if edges % 4 == 0 else 1
    valid = jnp.concatenate([jnp.ones((own,), F32), (halo_rows < own).astype(F32)])
    valid = valid.reshape(source_tiles, 1, TILE)
    valid = jnp.broadcast_to(jnp.concatenate([valid, valid], axis=2), (source_tiles, 8, width))
    per_edge = (edges, TILE, width)
    per_dest = (dest_tiles, TILE, width)
    per_source = (source_tiles, TILE, width)
    return pl.pallas_call(
        functools.partial(attend_kernel, dest_tiles, source_tiles, edges, unroll),
        out_shape=(
            jax.ShapeDtypeStruct((own, width), BF),
            jax.ShapeDtypeStruct((own + halo, width), BF),
            jax.ShapeDtypeStruct((own + halo, width), BF),
            jax.ShapeDtypeStruct((2, RELS, TILE, width), F32),
            jax.ShapeDtypeStruct((RELS, 1, width), F32),
        ),
        in_specs=[SMEM] * 2 + [VMEM] * 8,
        out_specs=(VMEM,) * 5,
        scratch_shapes=[
            pltpu.VMEM((own + halo, width), BF),
            pltpu.VMEM((own + halo, width), BF),
            pltpu.VMEM((2, RELS, width, width), BF),
            pltpu.VMEM(per_edge, BF),
            pltpu.VMEM(per_edge, BF),
            pltpu.VMEM(per_edge, F32),
            pltpu.VMEM(per_edge, F32),
            pltpu.VMEM(per_edge, F32),
            pltpu.VMEM(per_dest, F32),
            pltpu.VMEM(per_dest, F32),
            pltpu.VMEM(per_dest, F32),
            pltpu.VMEM(per_source, F32),
            pltpu.VMEM(per_source, F32),
        ],
        compiler_params=pltpu.CompilerParams(vmem_limit_bytes=48 * 1024 * 1024),
        name="attend",
    )(
        edge_tiles.reshape(-1),
        rel_prior.reshape(-1),
        queries,
        key_rows,
        value_rows,
        halo_keys,
        halo_values,
        grad_output,
        valid,
        rel_weight,
    )


def per_device(
    node_feats,
    node_types,
    queries,
    key_rows,
    value_rows,
    halo_keys,
    halo_values,
    halo_rows,
    edge_tiles,
    grad_output,
    proj_weight,
    rel_weight,
    rel_prior,
):
    own_count = node_feats.shape[0]
    halo_count = halo_keys.shape[0]
    local_width = queries.shape[1]
    query_grad, key_grad, value_grad, relation_grad, prior_grad = attend(
        queries,
        key_rows,
        value_rows,
        halo_keys,
        halo_values,
        halo_rows,
        grad_output,
        edge_tiles,
        rel_weight,
        rel_prior,
    )
    relation_grad = jnp.transpose(
        relation_grad.reshape(2, RELS, TILE, 2, TILE), (0, 1, 3, 2, 4)
    )
    prior_grad = jnp.sum(prior_grad.reshape(RELS, 2, TILE), axis=-1)
    outgoing = jnp.concatenate([key_grad[own_count:], value_grad[own_count:]], axis=1)
    incoming, incoming_rows = (
        lax.all_to_all(outgoing, "nodes", split_axis=0, concat_axis=0, tiled=True),
        lax.all_to_all(halo_rows, "nodes", split_axis=0, concat_axis=0, tiled=True),
    )
    type_range = jnp.arange(TYPES)
    own_types = (node_types[:, None] == type_range[None, :]).astype(BF)
    own_stack = jnp.stack([query_grad, key_grad[:own_count], value_grad[:own_count]], axis=1)
    own_blocks = own_types[:, None, :, None] * own_stack[:, :, None, :]
    clamped = jnp.minimum(incoming_rows, own_count - 1)
    halo_types = (node_types[clamped][:, None] == type_range[None, :]).astype(BF)
    halo_types = halo_types * (incoming_rows < own_count).astype(BF)[:, None]
    halo_blocks = (
        halo_types[:, None, :, None] * incoming.reshape(halo_count, 2, local_width)[:, :, None, :]
    )
    contract = (((1, 2, 3), (0, 1, 3)), ((), ()))
    feat_grad = lax.dot_general(own_blocks, proj_weight, contract, preferred_element_type=F32)
    halo_feat = lax.dot_general(halo_blocks, proj_weight[1:], contract, preferred_element_type=F32)
    feat_grad = feat_grad.at[incoming_rows].add(halo_feat, mode="drop")
    grad_feats = lax.psum_scatter(feat_grad, "heads", scatter_dimension=1, tiled=True).astype(BF)
    own_part = jnp.einsum("ri,rptk->iptk", node_feats, own_blocks, preferred_element_type=F32)
    halo_part = jnp.einsum(
        "ri,rptk->iptk", node_feats[clamped], halo_blocks, preferred_element_type=F32
    )
    grad_proj = lax.psum_scatter(
        own_part.at[:, 1:].add(halo_part), "nodes", scatter_dimension=0, tiled=True
    )
    grad_rel, grad_prior = lax.psum((relation_grad, prior_grad), "nodes")
    return (grad_feats, grad_proj, grad_rel, grad_prior)


def solution(mesh):
    return jax.shard_map(
        per_device,
        mesh=mesh,
        in_specs=(
            P("nodes", None),
            P("nodes"),
            P("nodes", "heads"),
            P("nodes", "heads"),
            P("nodes", "heads"),
            P("nodes", "heads"),
            P("nodes", "heads"),
            P("nodes"),
            P("nodes", None),
            P("nodes", "heads"),
            P(None, None, None, "heads"),
            P(None, None, "heads", None, None),
            P(None, "heads"),
        ),
        out_specs=(
            P("nodes", "heads"),
            P("nodes", None, None, "heads"),
            P(None, None, "heads", None, None),
            P(None, "heads"),
        ),
        check_vma=False,
    )
```

time: 346 us -> 331 us (0.957)
  matrix products: 55.5 us -> 8.78 us
  waiting for transfers between devices: 186 us -> 218 us
  Pallas kernels: 0 us -> 18.3 us
  local copies, waits for them, and re-layouts: 43.4 us -> 30.2 us
  other arithmetic: 11.1 us -> 5.64 us
    unnamed x2 -> x3, waiting for transfers between devices: 0.03 us -> 214 us
    psum x1 -> x0, waiting for transfers between devices: 182 us -> none  [per_device(): summed = lax.psum(own_part.at[:, 1:].add(halo_part), 'nodes')]
    dot_general x24 -> x1, matrix products: 50.4 us -> 3.95 us  [per_device(): jnp.einsum('ri,rptk->iptk', node_feats[clamped], halo_blocks, preferred_e...]
    pallas_call x0 -> x1, Pallas kernels: none -> 18.3 us  [attend(): pl.pallas_call(functools.partial(attend_kernel, dest_tiles, source_tiles,...]
    transpose x4 -> x0, local copies, waits for them, and re-layouts: 13.2 us -> none  [the longest x1 3.32 us: attend(): jnp.einsum('eshb,ehab->esha', message_grad, message_weight, preferred_ele...]
    gather x8 -> x1, local copies, waits for them, and re-layouts: 9.15 us -> 0.7 us  [per_device(): node_feats[clamped]]
    scatter-add x0 -> x1, local copies, waits for them, and re-layouts: none -> 6.6 us  [per_device(): own_part.at[:, 1:].add(halo_part)]
    unnamed x75 -> x34, local copies, waits for them, and re-layouts: 10.9 us -> 16.8 us
  transfers between devices with their start and end apart: 4 -> 4, of which waited for: 2 -> 2; matrix products, arithmetic and copies ran while one was open for 27% -> 8% of each run, Pallas kernels for 0% -> 6%
where the time goes in v1:
time: 331 us; the launch traced here: 330 us
  waiting for transfers between devices  218 us (66%)
  local copies, waits for them, and re-layouts  30.2 us (9%)
  blocking collectives  19 us (6%)
  Pallas kernels  18.3 us (6%)
  between operations  16.3 us (5%)
  starting transfers between devices  13.3 us (4%)
  matrix products  8.78 us (3%)
  other arithmetic  5.64 us (2%)
    unnamed x3, waiting for transfers between devices  214 us
    psum x1, blocking collectives, per_device(): grad_rel, grad_prior = lax.psum((relation_grad, prior_grad), 'nodes')  19 us
    pallas_call x1, Pallas kernels, attend(): pl.pallas_call(functools.partial(attend_kernel, dest_tiles, source_tiles,...  18.3 us
    unnamed x34, local copies, waits for them, and re-layouts  16.8 us
    all_to_all x1, starting transfers between devices, per_device(): lax.all_to_all(halo_rows, 'nodes', split_axis=0, concat_axis=0, tiled=True)  7.28 us
  transfers between devices with their start and end apart: 4, of which 2 were waited for; matrix products, arithmetic and copies ran while one was open for 8% of the time, Pallas kernels for 6%

profile of v1, /device:TPU:0, one launch (start us, length us, event | category | flops | bytes accessed | tf_op | source)
XLA Modules:
  0.0 329.8 jit_solution(7217573563470794961)
XLA Ops:
  8.0 1.4 all_to_all.14
  9.4 7.3 %all-to-all-start = ((s32[8,8,1]{1,2,0:T(1,128)}), s32[8,8,1]{1,2,0:T(1,128)S(1)}, u32[]{:S(2)}, u32[]{:S(2)}) async-start(s32[8,8,1]{1,2,0:T(1,128)} %bitcast.6), calls=%async_computation | async-start | bytes 8192 | tf_op jit(solution)/shard_map/all_to_all | solution.py:298
  17.5 0.8 copy.45
  18.4 0.8 copy.44
  19.3 1.2 copy-done.1
  20.5 0.8 copy-done.2
  21.3 0.8 copy-done.3
  22.1 0.8 copy-done.4
  23.0 0.8 copy-done.5
  23.8 0.7 copy-done.6
  24.5 0.7 copy-done.7
  25.3 18.3 %attend.1 = (bf16[256,128]{1,0:T(8,128)(2,1)S(1)}, bf16[320,128]{1,0:T(8,128)(2,1)S(1)}, bf16[320,128]{1,0:T(8,128)(2,1)S(1)}, f32[2,15,64,128]{3,2,1,0:T(8,128)S(1)}, f32[15,1,128]{2,1,0:T(1,128)S(1)}) custom-call(s32[120]{0:T(128)S(1)} %reshape.180.edge_ref, f32[30]{0:T(128)S(1)} %reshape.181.prior_ref, bf16[256,128]{1,0:T(8,128)(2,1)S(1)} %copy-done.2, ...), custom_call_target="tpu_custom_call" | custom-call | tf_op jit(solution)/shard_map/attend/pallas_call | solution.py:219
  43.6 0.7 fusion.26
  44.5 2.3 fusion.8
  47.4 6.0 %all-to-all-start.1 = ((bf16[8,8,256]{2,1,0:T(8,128)(2,1)}), bf16[8,8,256]{2,1,0:T(8,128)(2,1)S(1)}, u32[]{:S(2)}, u32[]{:S(2)}) async-start(bf16[8,8,256]{2,1,0:T(8,128)(2,1)} %maximum_bitcast_fusion), calls=%async_computation.1 | async-start | bytes 65536 | tf_op jit(solution)/shard_map/all_to_all | solution.py:297
  54.9 0.8 gather_fusion
  55.7 4.4 %all-to-all-done.1 = bf16[8,8,256]{2,1,0:T(8,128)(2,1)S(1)} async-done(((bf16[8,8,256]{2,1,0:T(8,128)(2,1)}), bf16[8,8,256]{2,1,0:T(8,128)(2,1)S(1)}, u32[]{:S(2)}, u32[]{:S(2)}) %all-to-all-start.1) | async-done | bytes 32800 | tf_op jit(solution)/shard_map/all_to_all | solution.py:297
  60.1 1.9 fusion.11
  62.0 1.2 scatter_fusion
  63.2 0.8 copy-done.10
  64.1 1.1 reshape.183
  65.2 1.5 copy.62
  67.4 1.8 copy-done.9
  69.3 1.9 copy.64
  71.9 4.0 %fusion.1 = f32[512,3,5,128]{0,3,2,1:T(8,128)} fusion(f32[512,3,5,128]{0,3,2,1:T(8,128)} %copy.64, f32[3,5,128,512]{3,2,1,0:T(8,128)} %copy-done.9, bf16[64,2,128]{2,0,1:T(8,128)(2,1)S(1)} %copy.49, bf16[64,5]{0,1:T(8,128)(2,1)S(1)} %fusion.28, bf16[64,512]{1,0:T(8,128)(2,1)S(1)} %gather_fusion.1), kind=kOutput, calls=%fused_computation.5 | convolution fusion | flops 84869120 | bytes 5341824 | tf_op jit(solution)/shard_map/ri,rptk->iptk/dot_general | solution.py:316
  75.9 6.6 %copy.51 = f32[512,3,5,128]{3,1,2,0:T(4,128)} copy(f32[512,3,5,128]{0,3,2,1:T(8,128)} %fusion.1) | data formatting | bytes 7864320 | tf_op jit(solution)/shard_map/scatter-add | solution.py:320
  82.7 19.0 %psum.15 = f32[15,2]{1,0:T(8,128)S(1)} all-reduce(f32[15,2]{1,0:T(8,128)S(1)} %reduce_sum.9), channel_id=1, replica_groups=mesh['nodes'=8,'heads'=4] {'nodes'}, use_global_device_ids=true, to_apply=%region_5.0 | all-reduce | flops 30 | bytes 240 | tf_op jit(solution)/shard_map/psum | solution.py:322
  103.6 1.5 convert_element_type.25
  105.2 213.7 %all-reduce.5.cloned.1.call-done = (f32[512,3,5,128]{3,1,2,0:T(4,128)}, f32[2,15,2,64,64]{4,3,2,1,0:T(8,128)}) async-done(((f32[512,3,5,128]{3,1,2,0:T(4,128)}, f32[2,15,2,64,64]{4,3,2,1,0:T(8,128)}), (f32[512,3,5,128]{3,1,2,0:T(4,128)}, f32[2,15,2,64,64]{4,3,2,1,0:T(8,128)})) %all-reduce.5.cloned.1.call-update) | async-done | bytes 4915216
  318.9 1.3 constant_dynamic-slice_fusion
  320.2 0.8 copy.53
  321.1 1.3 copy.67
  (53 shorter events, 6.2 us)
Async XLA Ops:
  8.0 58.7 %copy-start = (bf16[256,512]{1,0:T(8,128)(2,1)S(1)}, bf16[256,512]{1,0:T(8,128)(2,1)}, u32[]{:S(2)}) copy-start(bf16[256,512]{1,0:T(8,128)(2,1)} %param.15) | copy-start | bytes 786436
  9.4 38.1 %all-to-all-start = ((s32[8,8,1]{1,2,0:T(1,128)}), s32[8,8,1]{1,2,0:T(1,128)S(1)}, u32[]{:S(2)}, u32[]{:S(2)}) async-start(s32[8,8,1]{1,2,0:T(1,128)} %bitcast.6), calls=%async_computation | async-start | bytes 8192 | tf_op jit(solution)/shard_map/all_to_all | solution.py:298
  19.2 1.2 copy-start.1
  20.5 0.8 copy-start.2
  21.3 0.8 copy-start.3
  22.1 0.8 copy-start.4
  23.0 0.8 copy-start.5
  23.8 0.7 copy-start.6
  24.5 0.7 copy-start.7
  43.6 11.3 %copy-start.8 = (s32[256]{0:T(256)S(1)}, s32[256]{0:T(256)}, u32[]{:S(2)}) copy-start(s32[256]{0:T(256)} %param.16) | copy-start | bytes 3076
  47.4 12.7 %all-to-all-start.1 = ((bf16[8,8,256]{2,1,0:T(8,128)(2,1)}), bf16[8,8,256]{2,1,0:T(8,128)(2,1)S(1)}, u32[]{:S(2)}, u32[]{:S(2)}) async-start(bf16[8,8,256]{2,1,0:T(8,128)(2,1)} %maximum_bitcast_fusion), calls=%async_computation.1 | async-start | bytes 65536 | tf_op jit(solution)/shard_map/all_to_all | solution.py:297
  53.4 50.2 %reduce-scatter.2.cloned.1.call-start = ((), (), s32[]{:S(2)}) async-start(), calls=%async_computation.3 | async-start | bytes 655360 | tf_op jit(solution)/shard_map/reduce_scatter | solution.py:314
  63.2 0.8 copy-start.10
  64.0 254.9 %all-reduce.5.cloned.1.call-start = ((), (), s32[]{:S(2)}) async-start(), calls=%async_computation.4 | async-start | bytes 14417920
  67.4 1.9 copy-start.9
  82.4 19.9 %copy-start.12 = (u32[32]{0:T(128)S(1)}, u32[32]{0:T(128)}, u32[]{:S(2)}) copy-start(u32[32]{0:T(128)} %constant.47) | copy-start | bytes 388
  318.9 2.2 copy-start.11
Sparse Core Ops, SparseCore 0:
  64.1 19.0 reduce-scatter.1
Sparse Core Ops, SparseCore 1:
  82.6 236.3 all-reduce.4

commit v2 on v1

--- a/solution.py
+++ b/solution.py
@@ -37,10 +37,10 @@
     halo_value_ref,
     grad_ref,
     valid_ref,
+    slot_ref,
     weight_ref,
-    query_out,
-    key_out,
-    value_out,
+    pack_out,
+    halo_out,
     rel_out,
     prior_out,
     keys,
@@ -176,20 +176,33 @@
                 )
             )
         for dest, source, rel, prior_now, query_now, key_now, value_now, one, two in found:
-            prior_out[rel] += prior_now
+            prior_out[pl.ds(rel, 1)] += prior_now
             query_acc[dest] += query_now
             key_acc[source] += key_now
             value_acc[source] += value_now
-            rel_out[0, rel] += one
-            rel_out[1, rel] += two
+            rel_out[rel] += one
+            rel_out[RELS + rel] += two
         return carry
 
     lax.fori_loop(0, edge_count // unroll, grad_step, 0)
     for tile in range(dest_tiles):
-        query_out[tile * TILE : (tile + 1) * TILE] = query_acc[tile].astype(BF)
-    for tile in range(source_tiles):
-        key_out[tile * TILE : (tile + 1) * TILE] = key_acc[tile].astype(BF)
-        value_out[tile * TILE : (tile + 1) * TILE] = value_acc[tile].astype(BF)
+        pack_out[tile * TILE : (tile + 1) * TILE] = query_acc[tile].astype(BF)
+        at = own + tile * TILE
+        pack_out[at : at + TILE] = key_acc[tile].astype(BF)
+        at = 2 * own + tile * TILE
+        pack_out[at : at + TILE] = value_acc[tile].astype(BF)
+    empty = jnp.zeros((CAP, width), F32)
+    for owner in range(halo_out.shape[0]):
+        tile, at = dest_tiles + owner * CAP // TILE, owner * CAP % TILE
+        halo_out[owner] = jnp.concatenate(
+            [
+                key_acc[tile, at : at + CAP],
+                value_acc[tile, at : at + CAP],
+                slot_ref[owner * CAP : (owner + 1) * CAP],
+                empty,
+            ],
+            axis=0,
+        ).astype(BF)
 
 
 def attend(
@@ -203,6 +216,7 @@
     edge_tiles,
     rel_weight,
     rel_prior,
+    rel_blocks,
 ):
     own, width = queries.shape
     halo = halo_keys.shape[0]
@@ -213,20 +227,20 @@
     valid = jnp.concatenate([jnp.ones((own,), F32), (halo_rows < own).astype(F32)])
     valid = valid.reshape(source_tiles, 1, TILE)
     valid = jnp.broadcast_to(jnp.concatenate([valid, valid], axis=2), (source_tiles, 8, width))
+    slots = jnp.broadcast_to(halo_rows.astype(F32)[:, None], (halo, width))
     per_edge = (edges, TILE, width)
     per_dest = (dest_tiles, TILE, width)
     per_source = (source_tiles, TILE, width)
     return pl.pallas_call(
         functools.partial(attend_kernel, dest_tiles, source_tiles, edges, unroll),
         out_shape=(
-            jax.ShapeDtypeStruct((own, width), BF),
-            jax.ShapeDtypeStruct((own + halo, width), BF),
-            jax.ShapeDtypeStruct((own + halo, width), BF),
-            jax.ShapeDtypeStruct((2, RELS, TILE, width), F32),
-            jax.ShapeDtypeStruct((RELS, 1, width), F32),
+            jax.ShapeDtypeStruct((3 * own, width), BF),
+            jax.ShapeDtypeStruct((halo // CAP, 4 * CAP, width), BF),
+            jax.ShapeDtypeStruct((rel_blocks, TILE, width), F32),
+            jax.ShapeDtypeStruct((16, width), F32),
         ),
-        in_specs=[SMEM] * 2 + [VMEM] * 8,
-        out_specs=(VMEM,) * 5,
+        in_specs=[SMEM] * 2 + [VMEM] * 9,
+        out_specs=(VMEM,) * 4,
         scratch_shapes=[
             pltpu.VMEM((own + halo, width), BF),
             pltpu.VMEM((own + halo, width), BF),
@@ -254,11 +268,413 @@
         halo_values,
         grad_output,
         valid,
+        slots,
         rel_weight,
     )
 
 
+def exchange_kernel(
+    nodes,
+    heads,
+    shard,
+    pack_ref,
+    halo_ref,
+    rel_ref,
+    prior_ref,
+    feats_ref,
+    weight_ref,
+    types_ref,
+    feats_out,
+    proj_out,
+    rel_out,
+    prior_out,
+    pack,
+    left_in,
+    back_in,
+    back,
+    prior_in,
+    rel_send,
+    rel_in,
+    rel_half,
+    rel_half_bf,
+    rel_parts,
+    feat_acc,
+    feat_send,
+    feat_in,
+    acc,
+    part_send,
+    part_in,
+    halo_sems,
+    prior_sems,
+    left_sems,
+    pack_sems,
+    back_sems,
+    pair_sems,
+    split_sems,
+    spread_sems,
+    across_sems,
+    head_sems,
+    part_sems,
+):
+    lines = nodes // 2
+    node = lax.axis_index("nodes")
+    head = lax.axis_index("heads")
+    line = node // 2
+    side = node % 2
+    own = types_ref.shape[0]
+    width = pack.shape[2]
+    slots = CAP * nodes
+    half = rel_half.shape[0]
+    piece = half // lines
+    mesh = pl.DeviceIdType.MESH
+
+    barrier = pltpu.get_barrier_semaphore()
+    for step in range(1, nodes):
+        peer = (lax.rem(node + step, nodes), head)
+        pl.semaphore_signal(barrier, inc=1, device_id=peer, device_id_type=mesh)
+    for step in range(1, heads):
+        peer = (node, lax.rem(head + step, heads))
+        pl.semaphore_signal(barrier, inc=1, device_id=peer, device_id_type=mesh)
+
+    def copy(source, target, sems, index, to_node, to_head=None):
+        return pltpu.make_async_remote_copy(
+            src_ref=source,
+            dst_ref=target,
+            send_sem=sems.at[0, index],
+            recv_sem=sems.at[1, index],
+            device_id=(to_node, head if to_head is None else to_head),
+            device_id_type=mesh,
+        )
+
+    def at_line(where):
+        return where * 2 + side
+
+    def travel(buffer, sems, step, act):
+        block = line - step + 1
+
+        @pl.when((line + 1 < lines) & (block >= 0))
+        def _():
+            here = buffer.at[block]
+            act(
+                pltpu.make_async_remote_copy(
+                    src_ref=here,
+                    dst_ref=here,
+                    send_sem=sems.at[0, step],
+                    recv_sem=sems.at[1, step],
+                    device_id=(at_line(line + 1), head),
+                    device_id_type=mesh,
+                )
+            )
+
+        other = line + step - 1
+
+        @pl.when((line >= 1) & (other < lines))
+        def _():
+            here = buffer.at[other]
+            act(
+                pltpu.make_async_remote_copy(
+                    src_ref=here,
+                    dst_ref=here,
+                    send_sem=sems.at[2, step],
+                    recv_sem=sems.at[3, step],
+                    device_id=(at_line(line - 1), head),
+                    device_id_type=mesh,
+                )
+            )
+
+    def landed(buffer, sems, index, step, block):
+        here = buffer.at[block]
+        pltpu.make_async_remote_copy(
+            src_ref=here,
+            dst_ref=here,
+            send_sem=sems.at[0, step],
+            recv_sem=sems.at[index, step],
+            device_id=(lax.rem(node + 1, nodes), head),
+            device_id_type=mesh,
+        ).wait_recv()
+
+    def start(item):
+        item.start()
+
+    def wait_send(item):
+        item.wait_send()
+
+    pack[line] = pack_ref[...]
+    left_in[line] = feats_ref[line]
+    back_in[node] = halo_ref[node]
+    prior_in[node] = prior_ref[...]
+    rel_send[...] = rel_ref[pl.ds(pl.multiple_of((1 - side) * half, 16), half)].astype(BF)
+    pl.semaphore_wait(barrier, nodes + heads - 2)
+
+    halo_copies, prior_copies, left_copies = [], [], []
+    for step in range(1, nodes):
+        to = lax.rem(node + step, nodes)
+        halo_copies.append(copy(halo_ref.at[to], back_in.at[node], halo_sems, step, to))
+        halo_copies[-1].start()
+    pair = copy(rel_send, rel_in, pair_sems, 0, line * 2 + 1 - side)
+    pair.start()
+    travel(pack, pack_sems, 1, start)
+    for step in range(1, lines):
+        to = lax.rem(line + step, lines)
+        left_copies.append(
+            copy(feats_ref.at[to], left_in.at[line], left_sems, step, at_line(to))
+        )
+        left_copies[-1].start()
+    for step in range(1, nodes):
+        to = lax.rem(node + step, nodes)
+        prior_copies.append(copy(prior_ref, prior_in.at[node], prior_sems, step, to))
+        prior_copies[-1].start()
+
+    types = types_ref[...].astype(F32)
+    type_masks = [(types == float(kind)).astype(F32).astype(BF) for kind in range(TYPES)]
+    for group in range(3):
+        rows = pack_ref[group * own : (group + 1) * own]
+        total = sum(
+            mm(rows * type_masks[kind], weight_ref[group, kind], 1, 1) for kind in range(TYPES)
+        )
+        if group == 0:
+            feat_acc[...] = total
+        else:
+            feat_acc[...] += total
+
+    for item in halo_copies:
+        item.wait_recv()
+    returned = back_in[...].astype(F32)
+    key_back = returned[:, :CAP].reshape(slots, width).astype(BF)
+    value_back = returned[:, CAP : 2 * CAP].reshape(slots, width).astype(BF)
+    ids = returned[:, 2 * CAP : 3 * CAP].reshape(slots, width)
+    back[line, :slots] = key_back
+    back[line, slots : 2 * slots] = value_back
+    back[line, 2 * slots :] = ids.astype(BF)
+    travel(back, back_sems, 1, start)
+
+    def chosen(found):
+        wide = jnp.concatenate([found] * (own // width), axis=1)
+        place = lax.broadcasted_iota(jnp.int32, (slots, own), 1).astype(F32)
+        return (wide == place).astype(F32).astype(BF)
+
+    pick = chosen(ids)
+    feat_back = jnp.zeros((slots, feat_acc.shape[1]), F32)
+    for kind in range(TYPES):
+        kept = mm(pick, type_masks[kind], 1, 0).astype(BF)
+        feat_back += mm(key_back * kept, weight_ref[1, kind], 1, 1)
+        feat_back += mm(value_back * kept, weight_ref[2, kind], 1, 1)
+    upper = feat_back.astype(BF)
+    lower = (feat_back - upper.astype(F32)).astype(BF)
+    feat_acc[...] += mm(pick, upper, 0, 0) + mm(pick, lower, 0, 0)
+    for index in range(heads):
+        feat_send[index] = feat_acc[:, index * width : (index + 1) * width].astype(BF)
+    head_copies = []
+    for step in range(1, heads):
+        to = lax.rem(head + step, heads)
+        head_copies.append(copy(feat_send.at[to], feat_in.at[step], head_sems, step, node, to))
+        head_copies[-1].start()
+
+    pair.wait_recv()
+    own_half = rel_ref[pl.ds(pl.multiple_of(side * half, 16), half)]
+    rel_half[...] = own_half + rel_in[...].astype(F32)
+    rel_half_bf[...] = rel_half[...].astype(BF)
+    split_copies = []
+    for step in range(1, lines):
+        to = lax.rem(line + step, lines)
+        part = rel_half_bf.at[pl.ds(pl.multiple_of(to * piece, 16), piece)]
+        split_copies.append(copy(part, rel_parts.at[step], split_sems, step, at_line(to)))
+        split_copies[-1].start()
+
+    acc[...] = jnp.zeros_like(acc)
+
+    def gather_step(block):
+        rows = left_in[block]
+        kinds = rows[2 * shard : 2 * shard + 1].astype(F32)
+        feats = rows[: 2 * shard]
+        masked = jnp.concatenate(
+            [feats * (kinds == float(kind)).astype(F32).astype(BF) for kind in range(TYPES)],
+            axis=0,
+        )
+        right = jnp.concatenate(
+            [pack[block, group * own : (group + 1) * own] for group in range(3)], axis=1
+        )
+        acc[...] += mm(masked, right, 1, 0)
+        return masked
+
+    def return_step(block, masked):
+        pick_now = chosen(back[block, 2 * slots :].astype(F32))
+        taken = mm(masked, pick_now, 1, 1).astype(BF)
+        right = jnp.concatenate([back[block, :slots], back[block, slots : 2 * slots]], axis=1)
+        acc[:, width:] += mm(taken, right, 1, 0)
+
+    return_step(line, gather_step(line))
+
+    spread_copies, across_copies = [], []
+
+    def send_across(index, slot):
+        here = rel_out.at[side, slot]
+        across_copies.append(copy(here, here, across_sems, index, line * 2 + 1 - side))
+        across_copies[-1].start()
+
+    for item in left_copies:
+        item.wait_recv()
+    for step in range(1, lines):
+
+        @pl.when(line - step >= 0)
+        def _():
+            landed(pack, pack_sems, 1, step, line - step)
+
+        @pl.when(line + step < lines)
+        def _():
+            landed(pack, pack_sems, 3, step, line + step)
+
+        if step + 1 < lines:
+            travel(pack, pack_sems, step + 1, start)
+
+        @pl.when(line - step >= 0)
+        def _():
+            landed(back, back_sems, 1, step, line - step)
+
+        @pl.when(line + step < lines)
+        def _():
+            landed(back, back_sems, 3, step, line + step)
+
+        if step + 1 < lines:
+            travel(back, back_sems, step + 1, start)
+
+        if step == 1:
+            for item in split_copies:
+                item.wait_recv()
+            final = rel_half[pl.ds(pl.multiple_of(line * piece, 16), piece)]
+            for index in range(1, lines):
+                final = final + rel_parts[index].astype(F32)
+            rel_out[side, line] = final.astype(BF)
+            for index in range(1, lines):
+                to = lax.rem(line + index, lines)
+                here = rel_out.at[side, line]
+                spread_copies.append(copy(here, here, spread_sems, index, at_line(to)))
+                spread_copies[-1].start()
+            send_across(0, line)
+
+        @pl.when(line - step >= 0)
+        def _():
+            return_step(line - step, gather_step(line - step))
+
+        @pl.when(line + step < lines)
+        def _():
+            return_step(line + step, gather_step(line + step))
+
+    def share(of):
+        return [
+            acc[pl.ds(pl.multiple_of(kind * 2 * shard + of * shard, 8), shard)]
+            for kind in range(TYPES)
+        ]
+
+    extra = part_send.shape[0] - TYPES * shard
+    tail = [jnp.zeros((extra, acc.shape[1]), F32)] if extra else []
+    part_send[...] = jnp.concatenate(share(1 - side) + tail, axis=0).astype(BF)
+    part = copy(part_send, part_in, part_sems, 0, line * 2 + 1 - side)
+    part.start()
+
+    for index, item in enumerate(spread_copies):
+        item.wait_recv()
+        send_across(index + 1, lax.rem(line - index - 1 + lines, lines))
+
+    for item in head_copies:
+        item.wait_recv()
+    mine = feat_acc[:, :width] * (head == 0).astype(F32)
+    for index in range(1, heads):
+        block = feat_acc[:, index * width : (index + 1) * width]
+        mine = mine + block * (head == index).astype(F32)
+    for step in range(1, heads):
+        mine = mine + feat_in[step].astype(F32)
+    feats_out[...] = mine.astype(BF)
+    for item in prior_copies:
+        item.wait_recv()
+    total = prior_in[0]
+    for index in range(1, nodes):
+        total = total + prior_in[index]
+    first = lax.broadcasted_iota(jnp.int32, total.shape, 1) < TILE
+    one = jnp.sum(jnp.where(first, total, 0.0), axis=1, keepdims=True)
+    two = jnp.sum(jnp.where(first, 0.0, total), axis=1, keepdims=True)
+    prior_out[...] = jnp.where(first, one, two)
+
+    part.wait_recv()
+    other = part_in[...].astype(F32)
+    for kind, rows in enumerate(share(side)):
+        rows = rows + other[kind * shard : (kind + 1) * shard]
+        for group in range(3):
+            proj_out[group, kind] = rows[:, group * width : (group + 1) * width]
+    for item in across_copies:
+        item.wait_recv()
+
+    sent = halo_copies + prior_copies + left_copies + head_copies + split_copies
+    for item in sent + spread_copies + across_copies + [pair, part]:
+        item.wait_send()
+    for step in range(1, lines):
+        travel(pack, pack_sems, step, wait_send)
+        travel(back, back_sems, step, wait_send)
+
+
+def exchange(nodes, heads, pack, halo, rel, prior, feats, weight, types):
+    own = types.shape[0]
+    width = pack.shape[1]
+    lines = nodes // 2
+    features = weight.shape[2]
+    shard = features // nodes
+    half = rel.shape[0] // 2
+    piece = half // lines
+    slots = CAP * nodes
+    part_rows = -(-TYPES * shard // 16) * 16
+
+    def sems(*dims):
+        return pltpu.SemaphoreType.DMA(dims)
+
+    return pl.pallas_call(
+        functools.partial(exchange_kernel, nodes, heads, shard),
+        out_shape=(
+            jax.ShapeDtypeStruct((own, width), BF),
+            jax.ShapeDtypeStruct((3, TYPES, shard, width), F32),
+            jax.ShapeDtypeStruct((2, lines, piece, width), BF),
+            jax.ShapeDtypeStruct((16, width), F32),
+        ),
+        in_specs=[VMEM] * 7,
+        out_specs=(VMEM,) * 4,
+        scratch_shapes=[
+            pltpu.VMEM((lines, 3 * own, width), BF),
+            pltpu.VMEM((lines,) + feats.shape[1:], BF),
+            pltpu.VMEM((nodes, 4 * CAP, width), BF),
+            pltpu.VMEM((lines, 3 * slots, width), BF),
+            pltpu.VMEM((nodes, 16, width), F32),
+            pltpu.VMEM((half, width), BF),
+            pltpu.VMEM((half, width), BF),
+            pltpu.VMEM((half, width), F32),
+            pltpu.VMEM((half, width), BF),
+            pltpu.VMEM((lines, piece, width), BF),
+            pltpu.VMEM((own, features), F32),
+            pltpu.VMEM((heads, own, width), BF),
+            pltpu.VMEM((heads, own, width), BF),
+            pltpu.VMEM((TYPES * 2 * shard, 3 * width), F32),
+            pltpu.VMEM((part_rows, 3 * width), BF),
+            pltpu.VMEM((part_rows, 3 * width), BF),
+            sems(2, nodes),
+            sems(2, nodes),
+            sems(2, lines),
+            sems(4, lines),
+            sems(4, lines),
+            sems(2, 1),
+            sems(2, lines),
+            sems(2, lines),
+            sems(2, lines),
+            sems(2, heads),
+            sems(2, 1),
+        ],
+        compiler_params=pltpu.CompilerParams(
+            collective_id=0, has_side_effects=True, vmem_limit_bytes=56 * 1024 * 1024
+        ),
+        name="exchange",
+    )(pack, halo, rel, prior, feats, weight, types)
+
+
 def per_device(
+    nodes,
+    heads,
     node_feats,
     node_types,
     queries,
@@ -273,10 +689,13 @@
     rel_weight,
     rel_prior,
 ):
-    own_count = node_feats.shape[0]
-    halo_count = halo_keys.shape[0]
-    local_width = queries.shape[1]
-    query_grad, key_grad, value_grad, relation_grad, prior_grad = attend(
+    own, features = node_feats.shape
+    width = queries.shape[1]
+    lines = nodes // 2
+    shard = features // nodes
+    piece = -(-2 * RELS * TILE // nodes // 16) * 16
+    rel_rows = max(piece * nodes, 2 * RELS * TILE)
+    pack, halo, rel, prior = attend(
         queries,
         key_rows,
         value_rows,
@@ -287,45 +706,33 @@
         edge_tiles,
         rel_weight,
         rel_prior,
+        rel_rows // TILE,
     )
-    relation_grad = jnp.transpose(
-        relation_grad.reshape(2, RELS, TILE, 2, TILE), (0, 1, 3, 2, 4)
+    kinds = jnp.broadcast_to(node_types.astype(BF)[None, None, :], (lines, 16, own))
+    feats = node_feats.T.reshape(lines, 2 * shard, own)
+    feats = jnp.concatenate([feats, kinds], axis=1)
+    types = jnp.broadcast_to(node_types[:, None], (own, width))
+    grad_feats, proj, rel, prior = exchange(
+        nodes,
+        heads,
+        pack,
+        halo,
+        rel.reshape(rel_rows, width),
+        prior,
+        feats,
+        proj_weight,
+        types,
     )
-    prior_grad = jnp.sum(prior_grad.reshape(RELS, 2, TILE), axis=-1)
-    outgoing = jnp.concatenate([key_grad[own_count:], value_grad[own_count:]], axis=1)
-    incoming, incoming_rows = (
-        lax.all_to_all(outgoing, "nodes", split_axis=0, concat_axis=0, tiled=True),
-        lax.all_to_all(halo_rows, "nodes", split_axis=0, concat_axis=0, tiled=True),
-    )
-    type_range = jnp.arange(TYPES)
-    own_types = (node_types[:, None] == type_range[None, :]).astype(BF)
-    own_stack = jnp.stack([query_grad, key_grad[:own_count], value_grad[:own_count]], axis=1)
-    own_blocks = own_types[:, None, :, None] * own_stack[:, :, None, :]
-    clamped = jnp.minimum(incoming_rows, own_count - 1)
-    halo_types = (node_types[clamped][:, None] == type_range[None, :]).astype(BF)
-    halo_types = halo_types * (incoming_rows < own_count).astype(BF)[:, None]
-    halo_blocks = (
-        halo_types[:, None, :, None] * incoming.reshape(halo_count, 2, local_width)[:, :, None, :]
-    )
-    contract = (((1, 2, 3), (0, 1, 3)), ((), ()))
-    feat_grad = lax.dot_general(own_blocks, proj_weight, contract, preferred_element_type=F32)
-    halo_feat = lax.dot_general(halo_blocks, proj_weight[1:], contract, preferred_element_type=F32)
-    feat_grad = feat_grad.at[incoming_rows].add(halo_feat, mode="drop")
-    grad_feats = lax.psum_scatter(feat_grad, "heads", scatter_dimension=1, tiled=True).astype(BF)
-    own_part = jnp.einsum("ri,rptk->iptk", node_feats, own_blocks, preferred_element_type=F32)
-    halo_part = jnp.einsum(
-        "ri,rptk->iptk", node_feats[clamped], halo_blocks, preferred_element_type=F32
-    )
-    grad_proj = lax.psum_scatter(
-        own_part.at[:, 1:].add(halo_part), "nodes", scatter_dimension=0, tiled=True
-    )
-    grad_rel, grad_prior = lax.psum((relation_grad, prior_grad), "nodes")
+    grad_proj = jnp.transpose(proj, (2, 0, 1, 3))
+    rel = rel.reshape(rel_rows, width)[: 2 * RELS * TILE].astype(F32)
+    grad_rel = jnp.transpose(rel.reshape(2, RELS, TILE, 2, TILE), (0, 1, 3, 2, 4))
+    grad_prior = prior[:RELS, ::TILE]
     return (grad_feats, grad_proj, grad_rel, grad_prior)
 
 
 def solution(mesh):
     return jax.shard_map(
-        per_device,
+        functools.partial(per_device, mesh.shape["nodes"], mesh.shape["heads"]),
         mesh=mesh,
         in_specs=(
             P("nodes", None),

time: 331 us -> 97.2 us (0.29)
  waiting for transfers between devices: 218 us -> 0 us
  Pallas kernels: 18.3 us -> 74.1 us
  blocking collectives: 19 us -> 0 us
  between operations: 16.3 us -> 0.73 us
  starting transfers between devices: 13.3 us -> 0 us
  local copies, waits for them, and re-layouts: 30.2 us -> 18.8 us
  matrix products: 8.78 us -> 0 us
    unnamed x3 -> x0, waiting for transfers between devices: 214 us -> none
    pallas_call x0 -> x1, Pallas kernels: none -> 55.9 us  [exchange(): pl.pallas_call(functools.partial(exchange_kernel, nodes, heads, shard), o...]
    psum x1 -> x0, blocking collectives: 19 us -> none  [per_device(): grad_rel, grad_prior = lax.psum((relation_grad, prior_grad), 'nodes')]
    all_to_all x2 -> x0, starting transfers between devices: 13.3 us -> none  [the longest x1 7.28 us: per_device(): lax.all_to_all(halo_rows, 'nodes', split_axis=0, concat_axis=0, tiled=True)]
    dot_general x4 -> x0, matrix products: 8.78 us -> none  [the longest x1 3.95 us: per_device(): jnp.einsum('ri,rptk->iptk', node_feats[clamped], halo_blocks, preferred_e...]
    scatter-add x1 -> x0, local copies, waits for them, and re-layouts: 6.6 us -> none  [per_device(): own_part.at[:, 1:].add(halo_part)]
    unnamed x34 -> x31, local copies, waits for them, and re-layouts: 16.8 us -> 11.2 us
    transpose x0 -> x3, local copies, waits for them, and re-layouts: none -> 4.99 us  [the longest x2 3.91 us: per_device(): jnp.transpose(rel.reshape(2, RELS, TILE, 2, TILE), (0, 1, 3, 2, 4))]
  transfers between devices with their start and end apart: 4 -> 0, of which waited for: 2 -> 0; matrix products, arithmetic and copies ran while one was open for 8% -> 0% of each run, Pallas kernels for 6% -> 0%
where the time goes in v2:
time: 97.2 us; the launch traced here: 96.6 us
  Pallas kernels  74.1 us (76%)
  local copies, waits for them, and re-layouts  18.8 us (19%)
  other arithmetic  2.9 us (3%)
    pallas_call x1, Pallas kernels, exchange(): pl.pallas_call(functools.partial(exchange_kernel, nodes, heads, shard), o...  55.9 us
    pallas_call x1, Pallas kernels, attend(): pl.pallas_call(functools.partial(attend_kernel, dest_tiles, source_tiles,...  18.2 us
    unnamed x31, local copies, waits for them, and re-layouts  11.2 us
    transpose x2, local copies, waits for them, and re-layouts, per_device(): jnp.transpose(rel.reshape(2, RELS, TILE, 2, TILE), (0, 1, 3, 2, 4))  3.91 us

profile of v2, /device:TPU:0, one launch (start us, length us, event | category | flops | bytes accessed | tf_op | source)
XLA Modules:
  0.0 96.6 jit_solution(7231258280646215500)
XLA Ops:
  0.6 0.8 convert_element_type.13
  1.4 0.7 convert_element_type.12
  2.1 0.7 broadcast_compare_fusion
  2.7 0.1 reshape.34
  2.8 0.1 convert_bitcast_fusion
  2.9 0.8 copy.23
  3.7 0.1 reshape.33.prior_ref
  3.8 0.8 copy.22
  4.5 0.1 reshape.32.edge_ref
  4.7 0.1 broadcast_in_dim.32.slot_ref
  4.7 1.4 %broadcast_in_dim.34.types_ref = s32[256,128]{1,0:T(8,128)} broadcast(s32[256]{0:T(256)} %param.14), dimensions={0} | broadcast | bytes 132096 | tf_op jit(solution)/shard_map/broadcast_in_dim | solution.py:714
  6.2 1.1 %copy.24 = bf16[512,256]{1,0:T(8,128)(2,1)S(1)} copy(bf16[512,256]{0,1:T(8,128)(2,1)} %bitcast.15) | data formatting | bytes 524288 | tf_op jit(solution)/shard_map/transpose | solution.py:712
  7.3 0.7 pad_maximum_fusion.feats_ref
  8.0 0.8 copy-done.4
  8.8 0.8 copy-done.5
  9.7 0.8 copy-done.6
  10.5 0.8 copy-done.7
  11.4 0.7 copy-done.8
  12.1 0.7 copy-done.9
  12.8 18.2 %attend.1 = (bf16[768,128]{1,0:T(8,128)(2,1)S(1)}, bf16[8,32,128]{2,1,0:T(8,128)(2,1)S(1)}, f32[30,64,128]{2,1,0:T(8,128)S(1)}, f32[16,128]{1,0:T(8,128)S(1)}) custom-call(s32[120]{0:T(128)S(1)} %reshape.32.edge_ref, f32[30]{0:T(128)S(1)} %reshape.33.prior_ref, bf16[256,128]{1,0:T(8,128)(2,1)S(1)} %copy-done.4, bf16[256,128]{1,0:T(8,128)(2,1)S(1)} %copy-done.5, ...), custom_call_target="tpu_custom_call" | custom-call | tf_op jit(solution)/shard_map/attend/pallas_call | solution.py:234
  31.0 0.0 copy-start
  31.1 0.9 copy-done
  32.0 0.7 copy-done.2
  32.7 0.6 copy-done.3
  33.3 0.6 copy-done.10
  33.9 55.9 %exchange.1 = (bf16[256,128]{1,0:T(8,128)(2,1)}, f32[3,5,64,128]{3,2,1,0:T(8,128)}, bf16[2,4,240,128]{3,2,1,0:T(8,128)(2,1)}, f32[16,128]{1,0:T(8,128)}) custom-call(bf16[768,128]{1,0:T(8,128)(2,1)} %copy-done.2, bf16[8,32,128]{2,1,0:T(8,128)(2,1)} %copy-done.3, f32[1920,128]{1,0:T(8,128)} %bitcast.11, f32[16,128]{1,0:T(8,128)} %copy-done.10, ...), custom_call_target="tpu_custom_call" | custom-call | tf_op jit(solution)/shard_map/exchange/pallas_call | solution.py:629
  89.8 0.8 slice.3
  90.6 0.6 copy.26
  91.2 2.4 %reshape.38 = f32[2,15,64,2,64]{4,3,2,1,0:T(2,128)S(1)} reshape(bf16[2,4,240,128]{3,2,1,0:T(8,128)(2,1)} %get-tuple-element.18) | data formatting | bytes 1474560 | tf_op jit(solution)/shard_map/transpose | solution.py:728
  93.6 1.5 %copy.28 = f32[2,15,64,2,64]{4,2,3,1,0:T(8,128)} copy(f32[2,15,64,2,64]{4,3,2,1,0:T(2,128)S(1)} %reshape.38) | data formatting | bytes 1966080 | tf_op jit(solution)/shard_map/transpose | solution.py:728
  95.1 0.6 copy.31
  95.8 0.8 copy.32
  (18 shorter events, 0.0 us)
Async XLA Ops:
  0.6 7.4 %copy-start.1 = (bf16[2,15,2,64,64]{4,3,2,1,0:T(8,128)(2,1)S(1)}, bf16[2,15,2,64,64]{4,3,2,1,0:T(8,128)(2,1)}, u32[]{:S(2)}) copy-start(bf16[2,15,2,64,64]{4,3,2,1,0:T(8,128)(2,1)} %weight_ref.2) | copy-start | bytes 1474564
  8.0 0.8 copy-start.4
  8.8 0.8 copy-start.5
  9.7 0.8 copy-start.6
  10.5 0.8 copy-start.7
  11.4 0.7 copy-start.8
  12.1 0.7 copy-start.9
  31.0 0.9 copy-start
  32.0 0.7 copy-start.2
  32.7 0.6 copy-start.3
  33.3 0.6 copy-start.10
  93.6 1.6 %copy-start.12 = (bf16[256,128]{1,0:T(8,128)(2,1)S(1)}, bf16[256,128]{1,0:T(8,128)(2,1)}, u32[]{:S(2)}) copy-start(bf16[256,128]{1,0:T(8,128)(2,1)} %get-tuple-element.32) | copy-start | bytes 196612
  93.6 2.2 %copy-start.11 = (f32[3,5,64,128]{3,2,1,0:T(8,128)S(1)}, f32[3,5,64,128]{3,2,1,0:T(8,128)}, u32[]{:S(2)}) copy-start(f32[3,5,64,128]{3,2,1,0:T(8,128)} %get-tuple-element.17) | copy-start | bytes 1474564

commit v3 on v2

--- a/solution.py
+++ b/solution.py
@@ -15,6 +15,7 @@
 F32 = jnp.float32
 VMEM = pl.BlockSpec(memory_space=pltpu.VMEM)
 SMEM = pl.BlockSpec(memory_space=pltpu.SMEM)
+HBM = pl.BlockSpec(memory_space=pltpu.HBM)
 
 
 def mm(left, right, left_dim, right_dim):
@@ -30,19 +31,21 @@
     unroll,
     edge_ref,
     prior_ref,
-    query_ref,
-    key_ref,
-    value_ref,
-    halo_key_ref,
-    halo_value_ref,
-    grad_ref,
-    valid_ref,
     slot_ref,
-    weight_ref,
+    query_hbm,
+    key_hbm,
+    value_hbm,
+    halo_key_hbm,
+    halo_value_hbm,
+    grad_hbm,
+    weight_hbm,
     pack_out,
     halo_out,
     rel_out,
     prior_out,
+    query_ref,
+    grad_ref,
+    weight_ref,
     keys,
     values,
     wide,
@@ -56,13 +59,41 @@
     query_acc,
     key_acc,
     value_acc,
+    valid_ref,
+    load_sems,
 ):
     own = dest_tiles * TILE
+    halo = (source_tiles - dest_tiles) * TILE
     width = 2 * TILE
-    keys[:own] = key_ref[...]
-    keys[own:] = halo_key_ref[...]
-    values[:own] = value_ref[...]
-    values[own:] = halo_value_ref[...]
+    loads = [
+        pltpu.make_async_copy(source, target, load_sems.at[index])
+        for index, (source, target) in enumerate(
+            (
+                (weight_hbm, weight_ref),
+                (key_hbm, keys.at[:own]),
+                (halo_key_hbm, keys.at[own:]),
+                (value_hbm, values.at[:own]),
+                (halo_value_hbm, values.at[own:]),
+                (query_hbm, query_ref),
+                (grad_hbm, grad_ref),
+            )
+        )
+    ]
+    for load in loads:
+        load.start()
+    for ref in (sums, deltas, query_acc, key_acc, value_acc, rel_out, prior_out):
+        ref[...] = jnp.zeros_like(ref)
+    lane = lax.broadcasted_iota(jnp.int32, (8, width), 1) % TILE
+    for tile in range(dest_tiles):
+        valid_ref[tile] = jnp.ones((8, width), F32)
+    for tile in range(halo // TILE):
+        found = jnp.zeros((8, width), F32)
+        for index in range(TILE):
+            inside = jnp.where(slot_ref[tile * TILE + index] < own, 1.0, 0.0)
+            found = jnp.where(lane == index, inside, found)
+        valid_ref[dest_tiles + tile] = found
+    for load in loads:
+        load.wait()
     blank = jnp.zeros((TILE, TILE), BF)
     for side in range(2):
         for rel in range(RELS):
@@ -73,8 +104,6 @@
                 ],
                 axis=0,
             )
-    for ref in (sums, deltas, query_acc, key_acc, value_acc, rel_out, prior_out):
-        ref[...] = jnp.zeros_like(ref)
     first = lax.broadcasted_iota(jnp.int32, (TILE, width), 1) < TILE
     first_row = lax.broadcasted_iota(jnp.int32, (1, width), 1) < TILE
     low = first.astype(F32).astype(BF)
@@ -92,12 +121,12 @@
         return jnp.where(first, left, right)
 
     def entry(index):
-        target = edge_ref[3 * index]
+        target = edge_ref[index, 0]
         live = target < dest_tiles
         dest = jnp.minimum(target, dest_tiles - 1)
-        source = edge_ref[3 * index + 1]
-        rel = edge_ref[3 * index + 2]
-        prior = jnp.where(first_row, prior_ref[2 * rel], prior_ref[2 * rel + 1])
+        source = edge_ref[index, 1]
+        rel = edge_ref[index, 2]
+        prior = jnp.where(first_row, prior_ref[rel, 0], prior_ref[rel, 1])
         return live, dest, source, rel, prior
 
     def rows_of(tile):
@@ -192,13 +221,18 @@
         at = 2 * own + tile * TILE
         pack_out[at : at + TILE] = value_acc[tile].astype(BF)
     empty = jnp.zeros((CAP, width), F32)
+    slot_row = lax.broadcasted_iota(jnp.int32, (CAP, width), 0)
     for owner in range(halo_out.shape[0]):
+        rows = empty
+        for index in range(CAP):
+            row = slot_ref[owner * CAP + index].astype(F32)
+            rows = jnp.where(slot_row == index, row, rows)
         tile, at = dest_tiles + owner * CAP // TILE, owner * CAP % TILE
         halo_out[owner] = jnp.concatenate(
             [
                 key_acc[tile, at : at + CAP],
                 value_acc[tile, at : at + CAP],
-                slot_ref[owner * CAP : (owner + 1) * CAP],
+                rows,
                 empty,
             ],
             axis=0,
@@ -224,10 +258,6 @@
     dest_tiles = own // TILE
     source_tiles = (own + halo) // TILE
     unroll = 4 if edges % 4 == 0 else 1
-    valid = jnp.concatenate([jnp.ones((own,), F32), (halo_rows < own).astype(F32)])
-    valid = valid.reshape(source_tiles, 1, TILE)
-    valid = jnp.broadcast_to(jnp.concatenate([valid, valid], axis=2), (source_tiles, 8, width))
-    slots = jnp.broadcast_to(halo_rows.astype(F32)[:, None], (halo, width))
     per_edge = (edges, TILE, width)
     per_dest = (dest_tiles, TILE, width)
     per_source = (source_tiles, TILE, width)
@@ -239,9 +269,12 @@
             jax.ShapeDtypeStruct((rel_blocks, TILE, width), F32),
             jax.ShapeDtypeStruct((16, width), F32),
         ),
-        in_specs=[SMEM] * 2 + [VMEM] * 9,
+        in_specs=[SMEM] * 3 + [HBM] * 7,
         out_specs=(VMEM,) * 4,
         scratch_shapes=[
+            pltpu.VMEM((own, width), BF),
+            pltpu.VMEM((own, width), BF),
+            pltpu.VMEM(rel_weight.shape, BF),
             pltpu.VMEM((own + halo, width), BF),
             pltpu.VMEM((own + halo, width), BF),
             pltpu.VMEM((2, RELS, width, width), BF),
@@ -255,20 +288,21 @@
             pltpu.VMEM(per_dest, F32),
             pltpu.VMEM(per_source, F32),
             pltpu.VMEM(per_source, F32),
+            pltpu.VMEM((source_tiles, 8, width), F32),
+            pltpu.SemaphoreType.DMA((7,)),
         ],
-        compiler_params=pltpu.CompilerParams(vmem_limit_bytes=48 * 1024 * 1024),
+        compiler_params=pltpu.CompilerParams(vmem_limit_bytes=60 * 1024 * 1024),
         name="attend",
     )(
-        edge_tiles.reshape(-1),
-        rel_prior.reshape(-1),
+        edge_tiles,
+        rel_prior,
+        halo_rows,
         queries,
         key_rows,
         value_rows,
         halo_keys,
         halo_values,
         grad_output,
-        valid,
-        slots,
         rel_weight,
     )
 
@@ -282,7 +316,7 @@
     rel_ref,
     prior_ref,
     feats_ref,
-    weight_ref,
+    weight_hbm,
     types_ref,
     feats_out,
     proj_out,
@@ -304,9 +338,12 @@
     acc,
     part_send,
     part_in,
+    weight_ref,
+    local_sems,
     halo_sems,
     prior_sems,
     left_sems,
+    share_sems,
     pack_sems,
     back_sems,
     pair_sems,
@@ -321,7 +358,8 @@
     head = lax.axis_index("heads")
     line = node // 2
     side = node % 2
-    own = types_ref.shape[0]
+    own = feats_ref.shape[3]
+    cuts = feats_ref.shape[1]
     width = pack.shape[2]
     slots = CAP * nodes
     half = rel_half.shape[0]
@@ -399,8 +437,14 @@
     def wait_send(item):
         item.wait_send()
 
-    pack[line] = pack_ref[...]
-    left_in[line] = feats_ref[line]
+    loads = [
+        pltpu.make_async_copy(weight_hbm, weight_ref, local_sems.at[0]),
+        pltpu.make_async_copy(feats_ref.at[line], left_in.at[line], local_sems.at[1]),
+    ]
+    for load in loads:
+        load.start()
+    pack[line, : 3 * own] = pack_ref[...]
+    pack[line, 3 * own :] = types_ref[...]
     back_in[node] = halo_ref[node]
     prior_in[node] = prior_ref[...]
     rel_send[...] = rel_ref[pl.ds(pl.multiple_of((1 - side) * half, 16), half)].astype(BF)
@@ -416,16 +460,28 @@
     travel(pack, pack_sems, 1, start)
     for step in range(1, lines):
         to = lax.rem(line + step, lines)
-        left_copies.append(
-            copy(feats_ref.at[to], left_in.at[line], left_sems, step, at_line(to))
-        )
+        here, there = feats_ref.at[to], left_in.at[line]
+        if cuts > 1:
+            here, there = here.at[head], there.at[head]
+        left_copies.append(copy(here, there, left_sems, step, at_line(to)))
         left_copies[-1].start()
     for step in range(1, nodes):
         to = lax.rem(node + step, nodes)
         prior_copies.append(copy(prior_ref, prior_in.at[node], prior_sems, step, to))
         prior_copies[-1].start()
 
-    types = types_ref[...].astype(F32)
+    def kinds_of(block):
+        found = pack[block, 3 * own :].astype(F32)
+        return jnp.concatenate([found[row : row + 1] for row in range(own // width)], axis=1)
+
+    square = (own, own)
+    even = lax.broadcasted_iota(jnp.int32, square, 0) == lax.broadcasted_iota(
+        jnp.int32, square, 1
+    )
+    spread = jnp.where(even, kinds_of(line), 0.0).astype(BF)
+    types = mm(spread, jnp.ones((own, width), BF), 1, 0)
+    for load in loads:
+        load.wait()
     type_masks = [(types == float(kind)).astype(F32).astype(BF) for kind in range(TYPES)]
     for group in range(3):
         rows = pack_ref[group * own : (group + 1) * own]
@@ -470,6 +526,17 @@
         head_copies.append(copy(feat_send.at[to], feat_in.at[step], head_sems, step, node, to))
         head_copies[-1].start()
 
+    share_copies = []
+    for step, item in enumerate(left_copies, 1):
+        item.wait_recv()
+        if cuts > 1:
+            here = left_in.at[lax.rem(line - step + lines, lines), head]
+            for other in range(1, heads):
+                to = lax.rem(head + other, heads)
+                index = step * heads + other
+                share_copies.append(copy(here, here, share_sems, index, node, to))
+                share_copies[-1].start()
+
     pair.wait_recv()
     own_half = rel_ref[pl.ds(pl.multiple_of(side * half, 16), half)]
     rel_half[...] = own_half + rel_in[...].astype(F32)
@@ -484,9 +551,8 @@
     acc[...] = jnp.zeros_like(acc)
 
     def gather_step(block):
-        rows = left_in[block]
-        kinds = rows[2 * shard : 2 * shard + 1].astype(F32)
-        feats = rows[: 2 * shard]
+        feats = left_in[block].reshape(2 * shard, own)
+        kinds = kinds_of(block)
         masked = jnp.concatenate(
             [feats * (kinds == float(kind)).astype(F32).astype(BF) for kind in range(TYPES)],
             axis=0,
@@ -505,14 +571,14 @@
 
     return_step(line, gather_step(line))
 
-    spread_copies, across_copies = [], []
-
-    def send_across(index, slot):
+    def across(slot):
         here = rel_out.at[side, slot]
-        across_copies.append(copy(here, here, across_sems, index, line * 2 + 1 - side))
-        across_copies[-1].start()
-
-    for item in left_copies:
+        return copy(here, here, across_sems, slot, line * 2 + 1 - side)
+
+    def send_across(slot):
+        across(slot).start()
+
+    for item in share_copies:
         item.wait_recv()
     for step in range(1, lines):
 
@@ -545,12 +611,8 @@
             for index in range(1, lines):
                 final = final + rel_parts[index].astype(F32)
             rel_out[side, line] = final.astype(BF)
-            for index in range(1, lines):
-                to = lax.rem(line + index, lines)
-                here = rel_out.at[side, line]
-                spread_copies.append(copy(here, here, spread_sems, index, at_line(to)))
-                spread_copies[-1].start()
-            send_across(0, line)
+            travel(rel_out.at[side], spread_sems, 1, start)
+            send_across(line)
 
         @pl.when(line - step >= 0)
         def _():
@@ -572,9 +634,27 @@
     part = copy(part_send, part_in, part_sems, 0, line * 2 + 1 - side)
     part.start()
 
-    for index, item in enumerate(spread_copies):
-        item.wait_recv()
-        send_across(index + 1, lax.rem(line - index - 1 + lines, lines))
+    for step in range(1, lines):
+        behind, ahead = line - step, line + step
+
+        @pl.when(behind >= 0)
+        def _():
+            landed(rel_out.at[side], spread_sems, 1, step, behind)
+
+        @pl.when(ahead < lines)
+        def _():
+            landed(rel_out.at[side], spread_sems, 3, step, ahead)
+
+        if step + 1 < lines:
+            travel(rel_out.at[side], spread_sems, step + 1, start)
+
+        @pl.when(behind >= 0)
+        def _():
+            send_across(behind)
+
+        @pl.when(ahead < lines)
+        def _():
+            send_across(ahead)
 
     for item in head_copies:
         item.wait_recv()
@@ -601,19 +681,20 @@
         rows = rows + other[kind * shard : (kind + 1) * shard]
         for group in range(3):
             proj_out[group, kind] = rows[:, group * width : (group + 1) * width]
-    for item in across_copies:
-        item.wait_recv()
+    for slot in range(lines):
+        across(slot).wait()
 
     sent = halo_copies + prior_copies + left_copies + head_copies + split_copies
-    for item in sent + spread_copies + across_copies + [pair, part]:
+    for item in sent + share_copies + [pair, part]:
         item.wait_send()
     for step in range(1, lines):
         travel(pack, pack_sems, step, wait_send)
         travel(back, back_sems, step, wait_send)
+        travel(rel_out.at[side], spread_sems, step, wait_send)
 
 
 def exchange(nodes, heads, pack, halo, rel, prior, feats, weight, types):
-    own = types.shape[0]
+    own = feats.shape[3]
     width = pack.shape[1]
     lines = nodes // 2
     features = weight.shape[2]
@@ -634,10 +715,10 @@
             jax.ShapeDtypeStruct((2, lines, piece, width), BF),
             jax.ShapeDtypeStruct((16, width), F32),
         ),
-        in_specs=[VMEM] * 7,
+        in_specs=[VMEM] * 4 + [HBM] * 2 + [VMEM],
         out_specs=(VMEM,) * 4,
         scratch_shapes=[
-            pltpu.VMEM((lines, 3 * own, width), BF),
+            pltpu.VMEM((lines, 3 * own + 16, width), BF),
             pltpu.VMEM((lines,) + feats.shape[1:], BF),
             pltpu.VMEM((nodes, 4 * CAP, width), BF),
             pltpu.VMEM((lines, 3 * slots, width), BF),
@@ -653,20 +734,23 @@
             pltpu.VMEM((TYPES * 2 * shard, 3 * width), F32),
             pltpu.VMEM((part_rows, 3 * width), BF),
             pltpu.VMEM((part_rows, 3 * width), BF),
+            pltpu.VMEM(weight.shape, BF),
+            sems(2),
             sems(2, nodes),
             sems(2, nodes),
             sems(2, lines),
+            sems(2, lines * heads),
             sems(4, lines),
             sems(4, lines),
             sems(2, 1),
             sems(2, lines),
-            sems(2, lines),
+            sems(4, lines),
             sems(2, lines),
             sems(2, heads),
             sems(2, 1),
         ],
         compiler_params=pltpu.CompilerParams(
-            collective_id=0, has_side_effects=True, vmem_limit_bytes=56 * 1024 * 1024
+            collective_id=0, has_side_effects=True, vmem_limit_bytes=60 * 1024 * 1024
         ),
         name="exchange",
     )(pack, halo, rel, prior, feats, weight, types)
@@ -708,10 +792,10 @@
         rel_prior,
         rel_rows // TILE,
     )
-    kinds = jnp.broadcast_to(node_types.astype(BF)[None, None, :], (lines, 16, own))
-    feats = node_feats.T.reshape(lines, 2 * shard, own)
-    feats = jnp.concatenate([feats, kinds], axis=1)
-    types = jnp.broadcast_to(node_types[:, None], (own, width))
+    cuts = heads if 2 * shard % (16 * heads) == 0 else 1
+    feats = node_feats.T.reshape(lines, cuts, 2 * shard // cuts, own)
+    types = node_types.astype(BF).reshape(own // width, width)
+    types = jnp.pad(types, ((0, 16 - own // width), (0, 0)))
     grad_feats, proj, rel, prior = exchange(
         nodes,
         heads,

time: 97.2 us -> 81 us (0.83)
  local copies, waits for them, and re-layouts: 18.8 us -> 11.8 us
  Pallas kernels: 74.1 us -> 67.4 us
  other arithmetic: 2.9 us -> 0.68 us
    pallas_call x1, Pallas kernels: 55.9 us -> 46.3 us  [exchange(): pl.pallas_call(functools.partial(exchange_kernel, nodes, heads, shard), o...]
    unnamed x31 -> x9, local copies, waits for them, and re-layouts: 11.2 us -> 4.78 us
    pallas_call x1, Pallas kernels: 18.2 us -> 21.1 us  [attend(): pl.pallas_call(functools.partial(attend_kernel, dest_tiles, source_tiles,...]
    broadcast_in_dim x4 -> x0, local copies, waits for them, and re-layouts: 1.53 us -> none  [the longest x1 1.45 us: per_device(): types = jnp.broadcast_to(node_types[:, None], (own, width))]
    convert_element_type x2 -> x0, other arithmetic: 1.42 us -> none  [the longest x1 0.77 us: per_device(): node_types.astype(BF)[None, None, :]]
where the time goes in v3:
time: 81 us; the launch traced here: 80.6 us
  Pallas kernels  67.4 us (83%)
  local copies, waits for them, and re-layouts  11.8 us (15%)
    pallas_call x1, Pallas kernels, exchange(): pl.pallas_call(functools.partial(exchange_kernel, nodes, heads, shard), o...  46.3 us
    pallas_call x1, Pallas kernels, attend(): pl.pallas_call(functools.partial(attend_kernel, dest_tiles, source_tiles,...  21.1 us
    unnamed x9, local copies, waits for them, and re-layouts  4.78 us
    transpose x2, local copies, waits for them, and re-layouts, per_device(): jnp.transpose(rel.reshape(2, RELS, TILE, 2, TILE), (0, 1, 3, 2, 4))  3.91 us
    transpose x1, local copies, waits for them, and re-layouts, per_device(): feats = node_feats.T.reshape(lines, cuts, 2 * shard // cuts, own)  1.79 us

profile of v3, /device:TPU:0, one launch (start us, length us, event | category | flops | bytes accessed | tf_op | source)
XLA Modules:
  0.0 80.6 jit_solution(14490918031138887517)
XLA Ops:
  0.6 0.7 convert_bitcast_fusion
  1.3 0.6 pad.4.types_ref
  1.9 1.4 %copy.18.prior_ref = f32[15,2]{1,0:T(8,128)} copy(f32[15,2]{0,1:T(2,128)} %param.25) | data formatting | bytes 240 | tf_op args[12]
  3.3 1.4 %copy.17.edge_ref = s32[40,3]{1,0:T(8,128)} copy(s32[40,3]{0,1:T(4,128)} %param.21) | data formatting | bytes 960 | tf_op args[8]
  4.6 1.8 %copy.19 = bf16[512,256]{1,0:T(8,128)(2,1)} copy(bf16[512,256]{0,1:T(8,128)(2,1)} %bitcast.15) | data formatting | bytes 524288 | tf_op jit(solution)/shard_map/transpose | solution.py:796
  6.4 21.1 %attend.1 = (bf16[768,128]{1,0:T(8,128)(2,1)}, bf16[8,32,128]{2,1,0:T(8,128)(2,1)}, f32[30,64,128]{2,1,0:T(8,128)}, f32[16,128]{1,0:T(8,128)}) custom-call(s32[40,3]{1,0:T(8,128)} %copy.17.edge_ref, f32[15,2]{1,0:T(8,128)} %copy.18.prior_ref, s32[64]{0:T(128)} %slot_ref.1, bf16[256,128]{1,0:T(8,128)(2,1)} %query_hbm.1, bf16[256,128]{1,0:T(8,128)(2,1)} %key_hbm.1, ...), custom_call_target="tpu_custom_call" | custom-call | tf_op jit(solution)/shard_map/attend/pallas_call | solution.py:264
  27.5 46.3 %exchange.1 = (bf16[256,128]{1,0:T(8,128)(2,1)}, f32[3,5,64,128]{3,2,1,0:T(8,128)}, bf16[2,4,240,128]{3,2,1,0:T(8,128)(2,1)}, f32[16,128]{1,0:T(8,128)}) custom-call(bf16[768,128]{1,0:T(8,128)(2,1)} %get-tuple-element.12.pack_ref, bf16[8,32,128]{2,1,0:T(8,128)(2,1)} %get-tuple-element.13.halo_ref, f32[1920,128]{1,0:T(8,128)} %bitcast.13, ...), custom_call_target="tpu_custom_call" | custom-call | tf_op jit(solution)/shard_map/exchange/pallas_call | solution.py:710
  73.8 0.8 slice.3
  74.6 0.6 copy.21
  75.2 2.4 %reshape.25 = f32[2,15,64,2,64]{4,3,2,1,0:T(2,128)S(1)} reshape(bf16[2,4,240,128]{3,2,1,0:T(8,128)(2,1)} %get-tuple-element.18) | data formatting | bytes 1474560 | tf_op jit(solution)/shard_map/transpose | solution.py:812
  77.6 0.0 copy-start.1
  77.6 0.0 copy-start
  77.6 1.5 %copy.23 = f32[2,15,64,2,64]{4,2,3,1,0:T(8,128)} copy(f32[2,15,64,2,64]{4,3,2,1,0:T(2,128)S(1)} %reshape.25) | data formatting | bytes 1966080 | tf_op jit(solution)/shard_map/transpose | solution.py:812
  79.2 0.0 copy-done.1
  79.2 0.6 copy.26
  79.8 0.0 copy-done
  79.8 0.8 copy.27
Async XLA Ops:
  77.6 1.6 %copy-start.1 = (bf16[256,128]{1,0:T(8,128)(2,1)S(1)}, bf16[256,128]{1,0:T(8,128)(2,1)}, u32[]{:S(2)}) copy-start(bf16[256,128]{1,0:T(8,128)(2,1)} %get-tuple-element.28) | copy-start | bytes 196612
  77.6 2.2 %copy-start = (f32[3,5,64,128]{3,2,1,0:T(8,128)S(1)}, f32[3,5,64,128]{3,2,1,0:T(8,128)}, u32[]{:S(2)}) copy-start(f32[3,5,64,128]{3,2,1,0:T(8,128)} %get-tuple-element.17) | copy-start | bytes 1474564

commit v4 on v3

--- a/solution.py
+++ b/solution.py
@@ -121,12 +121,12 @@
         return jnp.where(first, left, right)
 
     def entry(index):
-        target = edge_ref[index, 0]
+        target = edge_ref[0, index]
         live = target < dest_tiles
         dest = jnp.minimum(target, dest_tiles - 1)
-        source = edge_ref[index, 1]
-        rel = edge_ref[index, 2]
-        prior = jnp.where(first_row, prior_ref[rel, 0], prior_ref[rel, 1])
+        source = edge_ref[1, index]
+        rel = edge_ref[2, index]
+        prior = jnp.where(first_row, prior_ref[0, rel], prior_ref[1, rel])
         return live, dest, source, rel, prior
 
     def rows_of(tile):
@@ -294,8 +294,8 @@
         compiler_params=pltpu.CompilerParams(vmem_limit_bytes=60 * 1024 * 1024),
         name="attend",
     )(
-        edge_tiles,
-        rel_prior,
+        edge_tiles.T,
+        rel_prior.T,
         halo_rows,
         queries,
         key_rows,
@@ -320,8 +320,9 @@
     types_ref,
     feats_out,
     proj_out,
+    rel_final,
+    prior_out,
     rel_out,
-    prior_out,
     pack,
     left_in,
     back_in,
@@ -444,7 +445,8 @@
     for load in loads:
         load.start()
     pack[line, : 3 * own] = pack_ref[...]
-    pack[line, 3 * own :] = types_ref[...]
+    blank = jnp.zeros((16 - own // width, width), F32)
+    pack[line, 3 * own :] = jnp.concatenate([types_ref[...].astype(F32), blank], axis=0).astype(BF)
     back_in[node] = halo_ref[node]
     prior_in[node] = prior_ref[...]
     rel_send[...] = rel_ref[pl.ds(pl.multiple_of((1 - side) * half, 16), half)].astype(BF)
@@ -578,6 +580,28 @@
     def send_across(slot):
         across(slot).start()
 
+    def spread_step(step):
+        behind, ahead = line - step, line + step
+
+        @pl.when(behind >= 0)
+        def _():
+            landed(rel_out.at[side], spread_sems, 1, step, behind)
+
+        @pl.when(ahead < lines)
+        def _():
+            landed(rel_out.at[side], spread_sems, 3, step, ahead)
+
+        if step + 1 < lines:
+            travel(rel_out.at[side], spread_sems, step + 1, start)
+
+        @pl.when(behind >= 0)
+        def _():
+            send_across(behind)
+
+        @pl.when(ahead < lines)
+        def _():
+            send_across(ahead)
+
     for item in share_copies:
         item.wait_recv()
     for step in range(1, lines):
@@ -603,6 +627,14 @@
 
         if step + 1 < lines:
             travel(back, back_sems, step + 1, start)
+
+        @pl.when(line - step >= 0)
+        def _():
+            return_step(line - step, gather_step(line - step))
+
+        @pl.when(line + step < lines)
+        def _():
+            return_step(line + step, gather_step(line + step))
 
         if step == 1:
             for item in split_copies:
@@ -613,14 +645,8 @@
             rel_out[side, line] = final.astype(BF)
             travel(rel_out.at[side], spread_sems, 1, start)
             send_across(line)
-
-        @pl.when(line - step >= 0)
-        def _():
-            return_step(line - step, gather_step(line - step))
-
-        @pl.when(line + step < lines)
-        def _():
-            return_step(line + step, gather_step(line + step))
+        else:
+            spread_step(step - 1)
 
     def share(of):
         return [
@@ -634,27 +660,7 @@
     part = copy(part_send, part_in, part_sems, 0, line * 2 + 1 - side)
     part.start()
 
-    for step in range(1, lines):
-        behind, ahead = line - step, line + step
-
-        @pl.when(behind >= 0)
-        def _():
-            landed(rel_out.at[side], spread_sems, 1, step, behind)
-
-        @pl.when(ahead < lines)
-        def _():
-            landed(rel_out.at[side], spread_sems, 3, step, ahead)
-
-        if step + 1 < lines:
-            travel(rel_out.at[side], spread_sems, step + 1, start)
-
-        @pl.when(behind >= 0)
-        def _():
-            send_across(behind)
-
-        @pl.when(ahead < lines)
-        def _():
-            send_across(ahead)
+    spread_step(lines - 1)
 
     for item in head_copies:
         item.wait_recv()
@@ -673,7 +679,8 @@
     first = lax.broadcasted_iota(jnp.int32, total.shape, 1) < TILE
     one = jnp.sum(jnp.where(first, total, 0.0), axis=1, keepdims=True)
     two = jnp.sum(jnp.where(first, 0.0, total), axis=1, keepdims=True)
-    prior_out[...] = jnp.where(first, one, two)
+    flipped = jnp.where(first, one, two).T
+    prior_out[...] = jnp.concatenate([flipped[:1], flipped[TILE : TILE + 1]], axis=0)
 
     part.wait_recv()
     other = part_in[...].astype(F32)
@@ -683,6 +690,14 @@
             proj_out[group, kind] = rows[:, group * width : (group + 1) * width]
     for slot in range(lines):
         across(slot).wait()
+    gathered = rel_out[...].astype(F32).reshape(2 * half, width)
+    for kind in range(2):
+        for rel in range(RELS):
+            at = (kind * RELS + rel) * TILE
+            for index in range(2):
+                rel_final[kind, rel, index] = gathered[
+                    at : at + TILE, index * TILE : (index + 1) * TILE
+                ]
 
     sent = halo_copies + prior_copies + left_copies + head_copies + split_copies
     for item in sent + share_copies + [pair, part]:
@@ -712,12 +727,13 @@
         out_shape=(
             jax.ShapeDtypeStruct((own, width), BF),
             jax.ShapeDtypeStruct((3, TYPES, shard, width), F32),
-            jax.ShapeDtypeStruct((2, lines, piece, width), BF),
-            jax.ShapeDtypeStruct((16, width), F32),
+            jax.ShapeDtypeStruct((2, RELS, 2, TILE, TILE), F32),
+            jax.ShapeDtypeStruct((2, 16), F32),
         ),
         in_specs=[VMEM] * 4 + [HBM] * 2 + [VMEM],
         out_specs=(VMEM,) * 4,
         scratch_shapes=[
+            pltpu.VMEM((2, lines, piece, width), BF),
             pltpu.VMEM((lines, 3 * own + 16, width), BF),
             pltpu.VMEM((lines,) + feats.shape[1:], BF),
             pltpu.VMEM((nodes, 4 * CAP, width), BF),
@@ -794,9 +810,8 @@
     )
     cuts = heads if 2 * shard % (16 * heads) == 0 else 1
     feats = node_feats.T.reshape(lines, cuts, 2 * shard // cuts, own)
-    types = node_types.astype(BF).reshape(own // width, width)
-    types = jnp.pad(types, ((0, 16 - own // width), (0, 0)))
-    grad_feats, proj, rel, prior = exchange(
+    types = node_types.reshape(own // width, width)
+    grad_feats, proj, grad_rel, prior = exchange(
         nodes,
         heads,
         pack,
@@ -808,9 +823,7 @@
         types,
     )
     grad_proj = jnp.transpose(proj, (2, 0, 1, 3))
-    rel = rel.reshape(rel_rows, width)[: 2 * RELS * TILE].astype(F32)
-    grad_rel = jnp.transpose(rel.reshape(2, RELS, TILE, 2, TILE), (0, 1, 3, 2, 4))
-    grad_prior = prior[:RELS, ::TILE]
+    grad_prior = prior[:, :RELS].T
     return (grad_feats, grad_proj, grad_rel, grad_prior)
 
 

time: 81 us -> 77.4 us (0.956)
  local copies, waits for them, and re-layouts: 11.8 us -> 9.4 us
    transpose x2 -> x1, local copies, waits for them, and re-layouts: 3.91 us -> 1.24 us  [per_device(): grad_prior = prior[:, :RELS].T]
    unnamed x9 -> x3, local copies, waits for them, and re-layouts: 4.78 us -> 6.37 us
where the time goes in v4:
time: 77.4 us; the launch traced here: 77.1 us
  Pallas kernels  67.1 us (87%)
  local copies, waits for them, and re-layouts  9.4 us (12%)
    pallas_call x1, Pallas kernels, exchange(): pl.pallas_call(functools.partial(exchange_kernel, nodes, heads, shard), o...  46.4 us
    pallas_call x1, Pallas kernels, attend(): pl.pallas_call(functools.partial(attend_kernel, dest_tiles, source_tiles,...  20.7 us
    unnamed x3, local copies, waits for them, and re-layouts  6.37 us
    transpose x1, local copies, waits for them, and re-layouts, per_device(): feats = node_feats.T.reshape(lines, cuts, 2 * shard // cuts, own)  1.79 us

profile of v4, /device:TPU:0, one launch (start us, length us, event | category | flops | bytes accessed | tf_op | source)
XLA Modules:
  0.0 77.1 jit_solution(3996037609948300850)
XLA Ops:
  0.6 1.8 %copy.17 = bf16[512,256]{1,0:T(8,128)(2,1)} copy(bf16[512,256]{0,1:T(8,128)(2,1)} %bitcast.12) | data formatting | bytes 524288 | tf_op jit(solution)/shard_map/transpose | solution.py:812
  2.4 20.7 %attend.1 = (bf16[768,128]{1,0:T(8,128)(2,1)}, bf16[8,32,128]{2,1,0:T(8,128)(2,1)}, f32[30,64,128]{2,1,0:T(8,128)}, f32[16,128]{1,0:T(8,128)}) custom-call(s32[3,40]{1,0:T(4,128)} %bitcast.13, f32[2,15]{1,0:T(2,128)} %bitcast.15, s32[64]{0:T(128)} %slot_ref.1, bf16[256,128]{1,0:T(8,128)(2,1)} %query_hbm.1, bf16[256,128]{1,0:T(8,128)(2,1)} %key_hbm.1, ...), custom_call_target="tpu_custom_call" | custom-call | tf_op jit(solution)/shard_map/attend/pallas_call | solution.py:264
  23.1 46.4 %exchange.1 = (bf16[256,128]{1,0:T(8,128)(2,1)}, f32[3,5,64,128]{3,2,1,0:T(8,128)}, f32[2,15,2,64,64]{4,3,2,1,0:T(8,128)}, f32[2,16]{1,0:T(2,128)}) custom-call(bf16[768,128]{1,0:T(8,128)(2,1)} %get-tuple-element.12.pack_ref, bf16[8,32,128]{2,1,0:T(8,128)(2,1)} %get-tuple-element.13.halo_ref, f32[1920,128]{1,0:T(8,128)} %bitcast.10, ...), custom_call_target="tpu_custom_call" | custom-call | tf_op jit(solution)/shard_map/exchange/pallas_call | solution.py:725
  69.5 1.2 %slice_bitcast_fusion = f32[15,2]{0,1:T(2,128)} fusion(f32[2,16]{1,0:T(2,128)} %get-tuple-element.19), kind=kLoop, calls=%fused_computation | loop fusion | bytes 240 | tf_op jit(solution)/shard_map/transpose | solution.py:826
  70.7 1.5 %copy.21 = bf16[256,128]{1,0:T(8,128)(2,1)} copy(bf16[256,128]{1,0:T(8,128)(2,1)} %get-tuple-element.24) | data formatting | bytes 131072
  72.2 1.9 %copy.22 = f32[64,3,5,128]{3,0,2,1:T(8,128)} copy(f32[64,3,5,128]{3,0,2,1:T(8,128)} %bitcast.11) | data formatting | bytes 983040
  74.1 3.0 %copy.23 = f32[2,15,2,64,64]{4,3,2,1,0:T(8,128)} copy(f32[2,15,2,64,64]{4,3,2,1,0:T(8,128)} %get-tuple-element.26) | data formatting | bytes 1966080

commit v5 on v4

--- a/solution.py
+++ b/solution.py
@@ -690,14 +690,7 @@
             proj_out[group, kind] = rows[:, group * width : (group + 1) * width]
     for slot in range(lines):
         across(slot).wait()
-    gathered = rel_out[...].astype(F32).reshape(2 * half, width)
-    for kind in range(2):
-        for rel in range(RELS):
-            at = (kind * RELS + rel) * TILE
-            for index in range(2):
-                rel_final[kind, rel, index] = gathered[
-                    at : at + TILE, index * TILE : (index + 1) * TILE
-                ]
+    rel_final[...] = rel_out[...]
 
     sent = halo_copies + prior_copies + left_copies + head_copies + split_copies
     for item in sent + share_copies + [pair, part]:
@@ -727,7 +720,7 @@
         out_shape=(
             jax.ShapeDtypeStruct((own, width), BF),
             jax.ShapeDtypeStruct((3, TYPES, shard, width), F32),
-            jax.ShapeDtypeStruct((2, RELS, 2, TILE, TILE), F32),
+            jax.ShapeDtypeStruct((2, lines, piece, width), BF),
             jax.ShapeDtypeStruct((2, 16), F32),
         ),
         in_specs=[VMEM] * 4 + [HBM] * 2 + [VMEM],
@@ -770,6 +763,36 @@
         ),
         name="exchange",
     )(pack, halo, rel, prior, feats, weight, types)
+
+
+def finish_kernel(feats_ref, proj_ref, rel_ref, prior_ref, feats_out, proj_out, rel_final, prior_out):
+    feats_out[...] = feats_ref[...]
+    proj_out[...] = proj_ref[...]
+    prior_out[...] = prior_ref[:, :RELS]
+    gathered = rel_ref[...].astype(F32).reshape(-1, rel_ref.shape[3])
+    for kind in range(2):
+        for rel in range(RELS):
+            at = (kind * RELS + rel) * TILE
+            for index in range(2):
+                rel_final[kind, rel, index] = gathered[
+                    at : at + TILE, index * TILE : (index + 1) * TILE
+                ]
+
+
+def finish(feats, proj, rel, prior):
+    return pl.pallas_call(
+        finish_kernel,
+        out_shape=(
+            jax.ShapeDtypeStruct(feats.shape, BF),
+            jax.ShapeDtypeStruct(proj.shape, F32),
+            jax.ShapeDtypeStruct((2, RELS, 2, TILE, TILE), F32),
+            jax.ShapeDtypeStruct((2, RELS), F32),
+        ),
+        in_specs=[VMEM] * 4,
+        out_specs=(VMEM,) * 4,
+        compiler_params=pltpu.CompilerParams(vmem_limit_bytes=60 * 1024 * 1024),
+        name="finish",
+    )(feats, proj, rel, prior)
 
 
 def per_device(
@@ -822,8 +845,9 @@
         proj_weight,
         types,
     )
+    grad_feats, proj, grad_rel, prior = finish(grad_feats, proj, grad_rel, prior)
     grad_proj = jnp.transpose(proj, (2, 0, 1, 3))
-    grad_prior = prior[:, :RELS].T
+    grad_prior = prior.T
     return (grad_feats, grad_proj, grad_rel, grad_prior)
 
 

time: 77.4 us -> 71.9 us (0.929)
  local copies, waits for them, and re-layouts: 9.4 us -> 1.79 us
  Pallas kernels: 67.1 us -> 69.3 us
    unnamed x3 -> x0, local copies, waits for them, and re-layouts: 6.37 us -> none
    pallas_call x0 -> x1, Pallas kernels: none -> 2.85 us  [finish(): pl.pallas_call(finish_kernel, out_shape=(jax.ShapeDtypeStruct(feats.shape...]
    transpose x1 -> x0, local copies, waits for them, and re-layouts: 1.24 us -> none  [per_device(): grad_prior = prior[:, :RELS].T]
where the time goes in v5:
time: 71.9 us; the launch traced here: 71.7 us
  Pallas kernels  69.3 us (96%)
  local copies, waits for them, and re-layouts  1.79 us (2%)
    pallas_call x1, Pallas kernels, exchange(): pl.pallas_call(functools.partial(exchange_kernel, nodes, heads, shard), o...  45.7 us
    pallas_call x1, Pallas kernels, attend(): pl.pallas_call(functools.partial(attend_kernel, dest_tiles, source_tiles,...  20.7 us
    pallas_call x1, Pallas kernels, finish(): pl.pallas_call(finish_kernel, out_shape=(jax.ShapeDtypeStruct(feats.shape...  2.85 us
    transpose x1, local copies, waits for them, and re-layouts, per_device(): feats = node_feats.T.reshape(lines, cuts, 2 * shard // cuts, own)  1.79 us

profile of v5, /device:TPU:0, one launch (start us, length us, event | category | flops | bytes accessed | tf_op | source)
XLA Modules:
  0.0 71.7 jit_solution(17836698917228529880)
XLA Ops:
  0.6 1.8 %copy.17 = bf16[512,256]{1,0:T(8,128)(2,1)} copy(bf16[512,256]{0,1:T(8,128)(2,1)} %bitcast.10) | data formatting | bytes 524288 | tf_op jit(solution)/shard_map/transpose | solution.py:835
  2.4 20.7 %attend.1 = (bf16[768,128]{1,0:T(8,128)(2,1)}, bf16[8,32,128]{2,1,0:T(8,128)(2,1)}, f32[30,64,128]{2,1,0:T(8,128)}, f32[16,128]{1,0:T(8,128)}) custom-call(s32[3,40]{1,0:T(4,128)} %bitcast.11, f32[2,15]{1,0:T(2,128)} %bitcast.13, s32[64]{0:T(128)} %slot_ref.1, bf16[256,128]{1,0:T(8,128)(2,1)} %query_hbm.1, bf16[256,128]{1,0:T(8,128)(2,1)} %key_hbm.1, ...), custom_call_target="tpu_custom_call" | custom-call | tf_op jit(solution)/shard_map/attend/pallas_call | solution.py:264
  23.1 45.7 %exchange.1 = (bf16[256,128]{1,0:T(8,128)(2,1)}, f32[3,5,64,128]{3,2,1,0:T(8,128)}, bf16[2,4,240,128]{3,2,1,0:T(8,128)(2,1)}, f32[2,16]{1,0:T(2,128)}) custom-call(bf16[768,128]{1,0:T(8,128)(2,1)} %get-tuple-element.16.pack_ref, bf16[8,32,128]{2,1,0:T(8,128)(2,1)} %get-tuple-element.17.halo_ref, f32[1920,128]{1,0:T(8,128)} %bitcast.9, ...), custom_call_target="tpu_custom_call" | custom-call | tf_op jit(solution)/shard_map/exchange/pallas_call | solution.py:718
  68.8 2.8 %finish.1 = (bf16[256,128]{1,0:T(8,128)(2,1)}, f32[3,5,64,128]{3,2,1,0:T(8,128)}, f32[2,15,2,64,64]{4,3,2,1,0:T(8,128)}, f32[2,15]{1,0:T(2,128)}) custom-call(bf16[256,128]{1,0:T(8,128)(2,1)} %get-tuple-element.20.feats_ref, f32[3,5,64,128]{3,2,1,0:T(8,128)} %get-tuple-element.21.proj_ref, bf16[2,4,240,128]{3,2,1,0:T(8,128)(2,1)} %get-tuple-element.22.rel_ref, ...), custom_call_target="tpu_custom_call" | custom-call | tf_op jit(solution)/shard_map/finish/pallas_call | solution.py:783
